TPU v7x, 512 devices: a whole 4x4x16 slice. The times are simulated.
512 devices in a mesh: member: 32 (over y_lo, z), fsdp: 16 (over x, y_hi, core).
Axes of the slice: x: 4, y: 4 (y_hi: 2, y_lo: 2; y = y_hi * 2 + y_lo), z: 16, core: 2. Of those that a mesh axis runs over, the one named last changes fastest.
Arguments:
- inputs: bfloat16 [32, 2048, 1792], P('member', 'fsdp'), may hold values from -6 to 6
- queries: bfloat16 [32, 2048, 2048], P('member', 'fsdp'), may hold values from -6 to 6
- keys: bfloat16 [32, 2048, 1024], P('member', 'fsdp'), may hold values from -6 to 6
- cotangent: bfloat16 [32, 2048, 2048], P('member', 'fsdp'), may hold values from -6 to 6
- winners: int32 [32], replicated, may hold values from 0 to 31, as said below
- weights: bfloat16 [32, 1792, 1024], P('member', 'fsdp'), may hold values from -0.125 to 0.125
- first_moment: float32 [32, 1792, 1024], P('member', 'fsdp'), may hold values from -4 to 4
- second_moment: float32 [32, 1792, 1024], P('member', 'fsdp'), may hold values from 0.001 to 1
Outputs:
- new_weights: bfloat16 [32, 1792, 1024], P('member', 'fsdp')
- new_first: float32 [32, 1792, 1024], P('member', 'fsdp')
- new_second: float32 [32, 1792, 1024], P('member', 'fsdp')
Inputs may be any that keep to these rules, and one draw needn't show every extreme that they name: winners[i] == i for the members that keep their state; the other 8 members name a member that keeps its own, and one member may be named by several.
All inputs are finite; a program needn't handle non-finite values.
Results may differ from a plain program's by a relative error of at most 0.015.
Values may be sent and summed in bfloat16 or wider, within the bound.
A program may use at most 64 MiB of HBM per device.

v0:
```python
import jax
import jax.numpy as jnp
from jax import lax
from jax.sharding import PartitionSpec as P

HEADS = 8
KV_HEADS = 4
HEAD_DIM = 256
SEQS = 1


beta_one = 0.9
beta_two = 0.999
learning_rate = 0.001
decay_rate = 0.1
adam_eps = 1e-08
adam_step = 200
soft_cap = 50.0


def local(inputs, queries, keys, cotangent, winners, weights, first_moment, second_moment):
    x_rows = inputs[0]
    k_rows = keys[0]
    tok_rows = x_rows.shape[0]
    feat_width = x_rows.shape[1]
    kv_width = k_rows.shape[1]
    groups = HEADS // KV_HEADS
    score_scale = HEAD_DIM ** (-0.5)
    fsdp_size = lax.axis_size("fsdp")
    fsdp_index = lax.axis_index("fsdp")
    seq_devices = fsdp_size // SEQS
    seq_len = seq_devices * tok_rows
    first_row = fsdp_index * tok_rows
    seq_begin = fsdp_index // seq_devices * seq_len
    query_heads = queries[0].reshape(tok_rows, KV_HEADS, groups, HEAD_DIM)
    grad_heads = cotangent[0].reshape(tok_rows, KV_HEADS, groups, HEAD_DIM)
    query_pos = first_row + jnp.arange(tok_rows, dtype=jnp.int32)
    start_state = (
        jnp.zeros((KV_HEADS, groups, tok_rows, feat_width), jnp.float32),
        jnp.zeros((KV_HEADS, groups, tok_rows), jnp.float32),
    )
    key_start = jnp.int32(0)
    x_piece = lax.all_gather(x_rows, "fsdp", axis=0, tiled=True)
    k_piece = lax.all_gather(k_rows, "fsdp", axis=0, tiled=True)
    key_count = x_piece.shape[0]
    key_pos = jnp.arange(key_count, dtype=jnp.int32)

    def compute(current):
        key_heads = k_piece.reshape(key_count, KV_HEADS, HEAD_DIM)
        scores = (
            jnp.einsum("rkgd,nkd->kgrn", query_heads, key_heads, preferred_element_type=jnp.float32)
            * score_scale
        )
        capped = soft_cap * jnp.tanh(scores / soft_cap)
        allowed = (key_pos[None, :] <= query_pos[:, None]) & (key_pos[None, :] >= seq_begin)
        weights_exp = jnp.where(allowed, jnp.exp(capped), jnp.zeros_like(capped))
        added = jnp.einsum(
            "kgrn,nc->kgrc",
            weights_exp.astype(jnp.bfloat16),
            x_piece,
            preferred_element_type=jnp.float32,
        )
        return (added, jnp.sum(weights_exp, axis=-1))

    needed = (key_start <= first_row + tok_rows - 1) & (key_start + key_count > seq_begin)
    running = lax.cond(needed, compute, lambda current: current, start_state)
    mixed = (running[0] / running[1][..., None]).astype(jnp.bfloat16)
    term = jnp.einsum("kgrc,rkgd->ckd", mixed, grad_heads, preferred_element_type=jnp.float32)
    gradient = (
        lax.psum_scatter(
            term.reshape(lax.axis_size("fsdp") * (feat_width // fsdp_size), kv_width).astype(
                jnp.bfloat16
            ),
            "fsdp",
            scatter_dimension=0,
            tiled=True,
        )
        .astype(jnp.float32)
        .reshape(weights.shape)
    )
    dealt_weights = lax.all_to_all(
        weights.reshape(1, -1), "member", split_axis=1, concat_axis=0, tiled=True
    )
    picked_weights = jnp.take(dealt_weights, winners, axis=0)
    source_weights = lax.all_to_all(
        picked_weights, "member", split_axis=0, concat_axis=1, tiled=True
    ).reshape(weights.shape)
    dealt_moments = (
        lax.all_to_all(
            first_moment.reshape(1, -1).astype(jnp.bfloat16),
            "member",
            split_axis=1,
            concat_axis=0,
            tiled=True,
        ).astype(jnp.float32),
        lax.all_to_all(
            second_moment.reshape(1, -1).astype(jnp.bfloat16),
            "member",
            split_axis=1,
            concat_axis=0,
            tiled=True,
        ).astype(jnp.float32),
    )
    picked_moments = (
        jnp.take(dealt_moments[0], winners, axis=0),
        jnp.take(dealt_moments[1], winners, axis=0),
    )
    moment_pair = (
        lax.all_to_all(
            picked_moments[0].astype(jnp.bfloat16),
            "member",
            split_axis=0,
            concat_axis=1,
            tiled=True,
        ).astype(jnp.float32),
        lax.all_to_all(
            picked_moments[1].astype(jnp.bfloat16),
            "member",
            split_axis=0,
            concat_axis=1,
            tiled=True,
        ).astype(jnp.float32),
    )
    source_first = moment_pair[0].reshape(weights.shape)
    source_second = moment_pair[1].reshape(weights.shape)
    new_first = beta_one * source_first + (1.0 - beta_one) * gradient
    new_second = beta_two * source_second + (1.0 - beta_two) * gradient * gradient
    first_hat = new_first / (1.0 - beta_one**adam_step)
    second_hat = new_second / (1.0 - beta_two**adam_step)
    source_float = source_weights.astype(jnp.float32)
    update = first_hat / (jnp.sqrt(second_hat) + adam_eps) + decay_rate * source_float
    new_weights = (source_float - learning_rate * update).astype(jnp.bfloat16)
    return (new_weights, new_first, new_second)


def solution(mesh):
    in_specs = (
        P("member", "fsdp", None),
        P("member", "fsdp", None),
        P("member", "fsdp", None),
        P("member", "fsdp", None),
        P(),
        P("member", "fsdp", None),
        P("member", "fsdp", None),
        P("member", "fsdp", None),
    )
    out_specs = (P("member", "fsdp", None), P("member", "fsdp", None), P("member", "fsdp", None))
    return jax.shard_map(local, mesh=mesh, in_specs=in_specs, out_specs=out_specs, check_vma=False)
```

profile of v0, /device:TPU:7, one launch (start us, length us, event | category | flops | bytes accessed | tf_op | source)
XLA Modules:
  0.0 345.3 jit_solution(11153914773508254086)
XLA Ops:
  8.6 1.0 convert_element_type.98
  10.4 2.0 reduce.6
  13.1 16.2 %all-to-all-start.2 = ((bf16[32,2,1792]{2,1,0:T(2,128)(2,1)}), bf16[32,2,1792]{2,1,0:T(2,128)(2,1)S(1)}, u32[]{:S(2)}, u32[]{:S(2)}) async-start(bf16[32,2,1792]{2,1,0:T(2,128)(2,1)} %reshape.213), calls=%async_computation.2 | async-start | bytes 458752 | tf_op jit(solution)/shard_map/all_to_all | solution.py:89
  29.4 1.3 copy.46
  30.7 57.5 %all-gather.5.cloned.1.call-done = bf16[1,2048,1024]{2,1,0:T(8,128)(2,1)} async-done(((bf16[1,128,1024]{2,1,0:T(8,128)(2,1)}), bf16[1,2048,1024]{2,1,0:T(8,128)(2,1)}) %all-gather.5.cloned.1.call-update) | async-done | bytes 4194320 | tf_op jit(solution)/shard_map/all_gather | solution.py:44
  88.2 85.2 %all-gather.7.cloned.1.call-done = bf16[1,2048,1792]{2,1,0:T(8,128)(2,1)} async-done(((bf16[1,128,1792]{2,1,0:T(8,128)(2,1)}), bf16[1,2048,1792]{2,1,0:T(8,128)(2,1)}) %all-gather.7.cloned.1.call-update) | async-done | bytes 7340048 | tf_op jit(solution)/shard_map/all_gather | solution.py:43
  173.4 28.2 %conditional.1 = (f32[4,2,128,1792]{3,2,1,0:T(8,128)}, f32[4,2,128]{2,1,0:T(2,128)S(1)}) conditional(s32[]{:T(128)} %convert_element_type.104, () %tuple.17, (s32[2048]{0:T(1024)S(1)}, s32[]{:T(128)}, s32[128]{0:T(128)S(1)}, s32[]{:T(128)}, s32[2048]{0:T(1024)S(1)}, /*index=5*/bf16[2048,1024]{1,0:T(8,128)(2,1)}, bf16[1,128,2048]{2,1,0:T(8,128)(2,1)}, ...), branch_computations={%region_0.2_spmd, %region_1.4_spmd} | conditional | flops 8607237120 | bytes 48522804 | solution.py:66
  173.4 1.5 compare_and_fusion
  174.9 7.9 %reshape.162 = bf16[2048,4,256]{2,1,0:T(4,128)(2,1)} reshape(bf16[2048,1024]{1,0:T(8,128)(2,1)} %get-tuple-element.24) | data formatting | bytes 8388608 | tf_op jit(solution)/shard_map/cond/branch_1_fun/reshape | solution.py:49
  183.1 4.7 %fusion.2 = (f32[4,2,128]{2,1,0:T(2,128)S(1)}, f32[4,2048,128,2]{2,1,3,0:T(8,128)S(1)}) fusion(pred[128,2048]{0,1:T(8,128)(4,1)S(1)} %compare_and_fusion, bf16[128,4,2,256]{3,2,1,0:T(2,128)(2,1)S(1)} %reshape_squeeze.5, bf16[2048,4,256,1]{2,1,0,3:T(4,128)(2,1)} %bitcast.56), kind=kOutput, calls=%fused_computation.6 | convolution fusion | flops 1082129408 | bytes 13373440 | tf_op jit(solution)/shard_map/cond/branch_1_fun/rkgd,nkd->kgrn/dot_general | solution.py:51
  187.9 13.7 %fusion = f32[4,2,128,1792]{3,2,1,0:T(8,128)} fusion(bf16[2048,1792]{1,0:T(8,128)(2,1)} %get-tuple-element.26, f32[4,2048,128,2]{2,1,3,0:T(8,128)S(1)} %get-tuple-element.37, pred[128,2048]{0,1:T(8,128)(4,1)S(1)} %compare_and_fusion), kind=kOutput, calls=%fused_computation.4 | convolution fusion | flops 7524581376 | bytes 23330816 | tf_op jit(solution)/shard_map/cond/branch_1_fun/kgrn,nc->kgrc/dot_general | solution.py:57
  201.6 6.1 %bitcast_convert_fusion = bf16[4,1792,256]{1,2,0:T(8,128)(2,1)} fusion(bf16[128,4,2,256]{0,3,2,1:T(8,128)(2,1)S(1)} %bitcast.64, f32[4,2,128,1792]{3,2,1,0:T(8,128)} %get-tuple-element.32, f32[4,2,128]{2,1,0:T(2,128)S(1)} %get-tuple-element.33), kind=kOutput, calls=%fused_computation.21 | convolution fusion | flops 945029120 | bytes 11538432 | tf_op jit(solution)/shard_map/kgrc,rkgd->ckd/dot_general | solution.py:68
  207.7 6.0 %copy.36 = bf16[1792,1024]{1,0:T(8,128)(2,1)} copy(bf16[1792,1024]{0,1:T(8,128)(2,1)} %bitcast.57) | data formatting | bytes 7340032 | tf_op jit(solution)/shard_map/convert_element_type | solution.py:71
  214.0 2.0 reduce.7
  216.7 12.3 %all-to-all-start.4 = ((bf16[32,2,1792]{2,1,0:T(2,128)(2,1)}), bf16[32,2,1792]{2,1,0:T(2,128)(2,1)S(1)}, u32[]{:S(2)}, u32[]{:S(2)}) async-start(bf16[32,2,1792]{2,1,0:T(2,128)(2,1)} %reshape.209), calls=%async_computation.5 | async-start | bytes 458752 | tf_op jit(solution)/shard_map/all_to_all | solution.py:96
  229.2 2.0 reduce.9
  232.2 16.0 %all-to-all-done.4 = bf16[32,2,1792]{2,1,0:T(2,128)(2,1)S(1)} async-done(((bf16[32,2,1792]{2,1,0:T(2,128)(2,1)}), bf16[32,2,1792]{2,1,0:T(2,128)(2,1)S(1)}, u32[]{:S(2)}, u32[]{:S(2)}) %all-to-all-start.4) | async-done | bytes 229408 | tf_op jit(solution)/shard_map/all_to_all | solution.py:96
  248.2 4.5 %all-to-all-start = ((bf16[32,2,1792]{2,1,0:T(2,128)(2,1)}), bf16[32,2,1792]{2,1,0:T(2,128)(2,1)S(1)}, u32[]{:S(2)}, u32[]{:S(2)}) async-start(bf16[32,2,1792]{2,1,0:T(2,128)(2,1)} %reshape.205), calls=%async_computation | async-start | bytes 458752 | tf_op jit(solution)/shard_map/all_to_all | solution.py:81
  255.2 0.7 reshape.215
  256.0 13.9 %all-to-all-done = bf16[32,2,1792]{2,1,0:T(2,128)(2,1)S(1)} async-done(((bf16[32,2,1792]{2,1,0:T(2,128)(2,1)}), bf16[32,2,1792]{2,1,0:T(2,128)(2,1)S(1)}, u32[]{:S(2)}, u32[]{:S(2)}) %all-to-all-start) | async-done | bytes 229408 | tf_op jit(solution)/shard_map/all_to_all | solution.py:81
  269.8 5.7 %all-to-all-start.3 = ((bf16[32,2,1792]{2,1,0:T(2,128)(2,1)}), bf16[32,2,1792]{2,1,0:T(2,128)(2,1)S(1)}, u32[]{:S(2)}, u32[]{:S(2)}) async-start(bf16[32,2,1792]{2,1,0:T(2,128)(2,1)} %reshape.215), calls=%async_computation.3 | async-start | bytes 458752 | tf_op jit(solution)/shard_map/all_to_all | solution.py:109
  276.3 0.7 reshape.211
  278.0 14.5 %all-to-all-done.3 = bf16[32,2,1792]{2,1,0:T(2,128)(2,1)S(1)} async-done(((bf16[32,2,1792]{2,1,0:T(2,128)(2,1)}), bf16[32,2,1792]{2,1,0:T(2,128)(2,1)S(1)}, u32[]{:S(2)}, u32[]{:S(2)}) %all-to-all-start.3) | async-done | bytes 229408 | tf_op jit(solution)/shard_map/all_to_all | solution.py:109
  292.4 5.1 %all-to-all-start.5 = ((bf16[32,2,1792]{2,1,0:T(2,128)(2,1)}), bf16[32,2,1792]{2,1,0:T(2,128)(2,1)S(1)}, u32[]{:S(2)}, u32[]{:S(2)}) async-start(bf16[32,2,1792]{2,1,0:T(2,128)(2,1)} %reshape.211), calls=%async_computation.6 | async-start | bytes 458752 | tf_op jit(solution)/shard_map/all_to_all | solution.py:116
  298.4 0.7 reshape.207
  299.1 15.0 %all-to-all-done.5 = bf16[32,2,1792]{2,1,0:T(2,128)(2,1)S(1)} async-done(((bf16[32,2,1792]{2,1,0:T(2,128)(2,1)}), bf16[32,2,1792]{2,1,0:T(2,128)(2,1)S(1)}, u32[]{:S(2)}, u32[]{:S(2)}) %all-to-all-start.5) | async-done | bytes 229408 | tf_op jit(solution)/shard_map/all_to_all | solution.py:116
  314.0 4.7 %all-to-all-start.1 = ((bf16[32,2,1792]{2,1,0:T(2,128)(2,1)}), bf16[32,2,1792]{2,1,0:T(2,128)(2,1)S(1)}, u32[]{:S(2)}, u32[]{:S(2)}) async-start(bf16[32,2,1792]{2,1,0:T(2,128)(2,1)} %reshape.207), calls=%async_computation.1 | async-start | bytes 458752 | tf_op jit(solution)/shard_map/all_to_all | solution.py:85
  319.0 1.4 multiply_reduce_fusion.1
  320.7 1.4 multiply_reduce_fusion
  322.3 12.6 %all-to-all-done.1 = bf16[32,2,1792]{2,1,0:T(2,128)(2,1)S(1)} async-done(((bf16[32,2,1792]{2,1,0:T(2,128)(2,1)}), bf16[32,2,1792]{2,1,0:T(2,128)(2,1)S(1)}, u32[]{:S(2)}, u32[]{:S(2)}) %all-to-all-start.1) | async-done | bytes 229408 | tf_op jit(solution)/shard_map/all_to_all | solution.py:85
  335.1 1.3 convert_reduce_fusion
  336.5 2.2 fusion.18
  (52 shorter events, 11.3 us)
Async XLA Ops:
  7.2 81.0 %all-gather.5.cloned.1.call-start = ((), (), s32[]{:S(2)}) async-start(), calls=%async_computation.8 | async-start | bytes 4456448 | tf_op jit(solution)/shard_map/all_gather | solution.py:44
  7.9 165.5 %all-gather.7.cloned.1.call-start = ((), (), s32[]{:S(2)}) async-start(), calls=%async_computation.9 | async-start | bytes 7798784 | tf_op jit(solution)/shard_map/all_gather | solution.py:43
  13.1 203.6 %all-to-all-start.2 = ((bf16[32,2,1792]{2,1,0:T(2,128)(2,1)}), bf16[32,2,1792]{2,1,0:T(2,128)(2,1)S(1)}, u32[]{:S(2)}, u32[]{:S(2)}) async-start(bf16[32,2,1792]{2,1,0:T(2,128)(2,1)} %reshape.213), calls=%async_computation.2 | async-start | bytes 458752 | tf_op jit(solution)/shard_map/all_to_all | solution.py:89
  29.3 307.2 %reduce-scatter.2.cloned.1.call-start = ((), (), s32[]{:S(2)}) async-start(), calls=%async_computation.7 | async-start | bytes 3899392 | tf_op jit(solution)/shard_map/reduce_scatter | solution.py:70
  173.4 9.4 %copy-start = (bf16[1,128,2048]{2,1,0:T(8,128)(2,1)S(1)}, bf16[1,128,2048]{2,1,0:T(8,128)(2,1)}, u32[]{:S(2)}) copy-start(bf16[1,128,2048]{2,1,0:T(8,128)(2,1)} %get-tuple-element.35) | copy-start | bytes 1572868 | tf_op jit(solution)/shard_map/cond
  207.7 6.1 %copy-start.1 = (f32[1,112,1024]{2,1,0:T(8,128)S(1)}, f32[1,112,1024]{2,1,0:T(8,128)}, u32[]{:S(2)}) copy-start(f32[1,112,1024]{2,1,0:T(8,128)} %param.19) | copy-start | bytes 1376260
  207.7 21.3 %copy-start.2 = (bf16[1,112,1024]{2,1,0:T(8,128)(2,1)S(1)}, bf16[1,112,1024]{2,1,0:T(8,128)(2,1)}, u32[]{:S(2)}) copy-start(bf16[1,112,1024]{2,1,0:T(8,128)(2,1)} %param.17) | copy-start | bytes 688132
  207.7 24.3 %copy-start.3 = (s32[32]{0:T(128)S(1)}, s32[32]{0:T(128)}, u32[]{:S(2)}) copy-start(s32[32]{0:T(128)} %param.16) | copy-start | bytes 388
  216.7 31.5 %all-to-all-start.4 = ((bf16[32,2,1792]{2,1,0:T(2,128)(2,1)}), bf16[32,2,1792]{2,1,0:T(2,128)(2,1)S(1)}, u32[]{:S(2)}, u32[]{:S(2)}) async-start(bf16[32,2,1792]{2,1,0:T(2,128)(2,1)} %reshape.209), calls=%async_computation.5 | async-start | bytes 458752 | tf_op jit(solution)/shard_map/all_to_all | solution.py:96
  248.2 21.6 %all-to-all-start = ((bf16[32,2,1792]{2,1,0:T(2,128)(2,1)}), bf16[32,2,1792]{2,1,0:T(2,128)(2,1)S(1)}, u32[]{:S(2)}, u32[]{:S(2)}) async-start(bf16[32,2,1792]{2,1,0:T(2,128)(2,1)} %reshape.205), calls=%async_computation | async-start | bytes 458752 | tf_op jit(solution)/shard_map/all_to_all | solution.py:81
  269.8 22.6 %all-to-all-start.3 = ((bf16[32,2,1792]{2,1,0:T(2,128)(2,1)}), bf16[32,2,1792]{2,1,0:T(2,128)(2,1)S(1)}, u32[]{:S(2)}, u32[]{:S(2)}) async-start(bf16[32,2,1792]{2,1,0:T(2,128)(2,1)} %reshape.215), calls=%async_computation.3 | async-start | bytes 458752 | tf_op jit(solution)/shard_map/all_to_all | solution.py:109
  292.4 21.6 %all-to-all-start.5 = ((bf16[32,2,1792]{2,1,0:T(2,128)(2,1)}), bf16[32,2,1792]{2,1,0:T(2,128)(2,1)S(1)}, u32[]{:S(2)}, u32[]{:S(2)}) async-start(bf16[32,2,1792]{2,1,0:T(2,128)(2,1)} %reshape.211), calls=%async_computation.6 | async-start | bytes 458752 | tf_op jit(solution)/shard_map/all_to_all | solution.py:116
  314.0 20.8 %all-to-all-start.1 = ((bf16[32,2,1792]{2,1,0:T(2,128)(2,1)}), bf16[32,2,1792]{2,1,0:T(2,128)(2,1)S(1)}, u32[]{:S(2)}, u32[]{:S(2)}) async-start(bf16[32,2,1792]{2,1,0:T(2,128)(2,1)} %reshape.207), calls=%async_computation.1 | async-start | bytes 458752 | tf_op jit(solution)/shard_map/all_to_all | solution.py:85
Sparse Core Ops, SparseCore 0:
  11.3 76.8 all-gather.4
  91.5 81.8 all-gather.6
  213.9 98.5 reduce-scatter.1
where the time goes:
time: 352 us; the launch traced here: 345 us
  waiting for transfers between devices  216 us (61%)
  starting transfers between devices  48.7 us (14%)
  local copies, waits for them, and re-layouts  24.6 us (7%)
  matrix products  24.5 us (7%)
  other arithmetic  17.4 us (5%)
  between operations  14 us (4%)
    all_gather x1, waiting for transfers between devices, local(): x_piece = lax.all_gather(x_rows, 'fsdp', axis=0, tiled=True)  85.2 us
    all_gather x1, waiting for transfers between devices, local(): k_piece = lax.all_gather(k_rows, 'fsdp', axis=0, tiled=True)  57.5 us
    all_to_all x1, starting transfers between devices, local(): lax.all_to_all(first_moment.reshape(1, -1).astype(jnp.bfloat16), 'member'...  16.2 us
    all_to_all x1, waiting for transfers between devices, local(): lax.all_to_all(second_moment.reshape(1, -1).astype(jnp.bfloat16), 'member...  16 us
    all_to_all x1, waiting for transfers between devices, local(): lax.all_to_all(picked_moments[1].astype(jnp.bfloat16), 'member', split_ax...  15 us
    all_to_all x1, waiting for transfers between devices, local(): lax.all_to_all(picked_moments[0].astype(jnp.bfloat16), 'member', split_ax...  14.5 us
    all_to_all x1, waiting for transfers between devices, local(): lax.all_to_all(weights.reshape(1, -1), 'member', split_axis=1, concat_axi...  13.9 us
    dot_general x1, matrix products, compute(): jnp.einsum('kgrn,nc->kgrc', weights_exp.astype(jnp.bfloat16), x_piece, pr...  13.7 us
  transfers between devices with their start and end apart: 9, of which 7 were waited for; matrix products, arithmetic and copies ran while one was open for 19% of the time, Pallas kernels for 0%

commit v1 on v0

v1 whole, which is shorter than its diff:
```python
import jax
import jax.numpy as jnp
from jax import lax
from jax.experimental import pallas as pl
from jax.experimental.pallas import tpu as pltpu
from jax.sharding import PartitionSpec as P

MEMBERS = 32
KV_HEADS = 4
QUARTERS = 4
HEAD_DIM = 256
GROUP_HEADS = 2
TOK = 128
FEAT = 1792
ROWS = 112
KVW = 1024
PART = QUARTERS * TOK
PIECE = 48
BANDS = 7

beta_one = 0.9
beta_two = 0.999
learning_rate = 0.001
decay_rate = 0.1
adam_eps = 1e-08
adam_step = 200
soft_cap = 50.0

MESH = pl.DeviceIdType.MESH


def kernel(
    winners, x_in, q_in, k_in, c_in, w_in, m_in, v_in,
    new_w, new_m, new_v,
    k_all, q_g, c_g, x_g, x_t, expo, denom, cots,
    dv_acc, dv_out, dv_in, gr_acc, gr_out, gr_in, sum_out, grad,
    state, dealt, picked, source,
    loc_sem, grp_send, grp_recv, key_send, key_recv, dv_send, dv_recv,
    gr_send, gr_recv, own_send, own_recv, deal_send, deal_recv, pick_send, pick_recv,
):
    me = lax.axis_index("member")
    mine = lax.axis_index("fsdp")
    j = mine // KV_HEADS
    g = mine % KV_HEADS

    barrier = pltpu.get_barrier_semaphore()
    for s in range(1, 4):
        pl.semaphore_signal(
            barrier, inc=1, device_id={"fsdp": j * 4 + (g + s) % 4}, device_id_type=MESH
        )
        pl.semaphore_signal(
            barrier, inc=1, device_id={"fsdp": (j + s) % 4 * 4 + g}, device_id_type=MESH
        )

    @pl.loop(1, MEMBERS)
    def _(s):
        pl.semaphore_signal(
            barrier, inc=1, device_id={"member": (me + s) % MEMBERS}, device_id_type=MESH
        )

    def own_slot(kind, owner):
        rows = pl.ds(owner * TOK, TOK)
        return (k_all.at[j, rows], q_g.at[rows], c_g.at[rows], x_g.at[rows])[kind]

    def own_slice(kind, head):
        if kind == 0:
            return k_in.at[:, pl.ds(head * HEAD_DIM, HEAD_DIM)]
        if kind == 3:
            return x_in
        wide = GROUP_HEADS * HEAD_DIM
        return (q_in, c_in)[kind - 1].at[:, pl.ds(head * wide, wide)]

    def group_copy(kind, s):
        peer = (g + s) % 4
        return pltpu.make_async_remote_copy(
            src_ref=own_slice(kind, peer),
            dst_ref=own_slot(kind, g),
            send_sem=grp_send.at[kind, s],
            recv_sem=grp_recv.at[kind, s],
            device_id={"fsdp": j * 4 + peer},
            device_id_type=MESH,
        )

    def group_wait(kind):
        for s in range(1, 4):
            slot = own_slot(kind, (g + 4 - s) % 4)
            pltpu.make_async_remote_copy(
                src_ref=slot,
                dst_ref=slot,
                send_sem=grp_send.at[kind, s],
                recv_sem=grp_recv.at[kind, s],
                device_id={"fsdp": j * 4 + (g + s) % 4},
                device_id_type=MESH,
            ).wait_recv()
        local_copy(kind).wait()

    def local_copy(kind):
        return pltpu.make_async_copy(own_slice(kind, g), own_slot(kind, g), loc_sem.at[kind])

    for kind in range(4):
        local_copy(kind).start()

    for band in range(4):
        cols = slice(band * 256, (band + 1) * 256)
        state[band, 0:ROWS] = w_in[:, cols]
        state[band, ROWS : 2 * ROWS] = m_in[:, cols].astype(jnp.bfloat16)
        state[band, 2 * ROWS : 3 * ROWS] = v_in[:, cols].astype(jnp.bfloat16)

    pl.semaphore_wait(barrier, 6 + MEMBERS - 1)

    for kind in range(3):
        for s in range(1, 4):
            group_copy(kind, s).start()

    sorts = me % 8 != BANDS

    def place(ref, member):
        return ref.at[member // 8, pl.ds(member % 8 * PIECE, PIECE)]

    def deal_copy(s):
        peer = (me + s) % MEMBERS
        return pltpu.make_async_remote_copy(
            src_ref=place(state, peer),
            dst_ref=dealt.at[me],
            send_sem=deal_send.at[s],
            recv_sem=deal_recv.at[s],
            device_id={"member": peer},
            device_id_type=MESH,
        )

    @pl.loop(1, MEMBERS)
    def _(s):
        @pl.when((me + s) % 8 != BANDS)
        def _():
            deal_copy(s).start()

    for s in range(1, 4):
        group_copy(3, s).start()

    @pl.when(sorts)
    def _():
        dealt[me] = state[me // 8, pl.ds(me % 8 * PIECE, PIECE)]

    def key_copy(s):
        return pltpu.make_async_remote_copy(
            src_ref=k_all.at[j],
            dst_ref=k_all.at[j],
            send_sem=key_send.at[s],
            recv_sem=key_recv.at[s],
            device_id={"fsdp": (j + s) % 4 * 4 + g},
            device_id_type=MESH,
        )

    def key_wait(s):
        slot = k_all.at[(j + 4 - s) % 4]
        pltpu.make_async_remote_copy(
            src_ref=slot,
            dst_ref=slot,
            send_sem=key_send.at[s],
            recv_sem=key_recv.at[s],
            device_id={"fsdp": (j + s) % 4 * 4 + g},
            device_id_type=MESH,
        ).wait_recv()

    group_wait(0)
    for s in range(1, 4):

        @pl.when(j + s < 4)
        def _(s=s):
            key_copy(s).start()

    group_wait(1)
    denom[...] = jnp.zeros_like(denom)

    def scores(chunk, diagonal):
        @pl.loop(0, 4)
        def _(block):
            first = pl.multiple_of(block * TOK, TOK)
            key_block = k_all[chunk, pl.ds(first, TOK), :]
            for h in range(GROUP_HEADS):
                raw = lax.dot_general(
                    key_block,
                    q_g[:, h * HEAD_DIM : (h + 1) * HEAD_DIM],
                    (((1,), (1,)), ((), ())),
                    preferred_element_type=jnp.float32,
                )
                e = jnp.exp(soft_cap * jnp.tanh(raw * (HEAD_DIM**-0.5 / soft_cap)))
                if diagonal:
                    u = first + lax.broadcasted_iota(jnp.int32, (TOK, PART), 0)
                    t = lax.broadcasted_iota(jnp.int32, (TOK, PART), 1)
                    e = jnp.where(u <= t, e, 0.0)
                cols = slice(h * PART, (h + 1) * PART)
                expo[chunk, pl.ds(first, TOK), cols] = e.astype(jnp.bfloat16)
                denom[:, cols] += jnp.sum(e, axis=0, keepdims=True)

    scores(j, True)
    for s in range(1, 4):

        @pl.when(j >= s)
        def _(s=s):
            key_wait(s)
            scores(j - s, False)

    group_wait(2)
    for h in range(GROUP_HEADS):
        cols = slice(h * PART, (h + 1) * PART)
        inverse = jnp.transpose(jnp.broadcast_to(1.0 / denom[:, cols], (128, PART)))
        heads = c_g[:, h * HEAD_DIM : (h + 1) * HEAD_DIM].astype(jnp.float32)
        for half in range(2):
            lanes = slice(half * 128, (half + 1) * 128)
            cots[cols, lanes] = (heads[:, lanes] * inverse).astype(jnp.bfloat16)

    def dv_copy(s):
        return pltpu.make_async_remote_copy(
            src_ref=dv_out.at[s],
            dst_ref=dv_in.at[s],
            send_sem=dv_send.at[s],
            recv_sem=dv_recv.at[s],
            device_id={"fsdp": (j + 4 - s) % 4 * 4 + g},
            device_id_type=MESH,
        )

    for s in range(1, 4):

        @pl.when(j >= s)
        def _(s=s):
            dv_out[s] = jnp.dot(
                expo[j - s], cots[...], preferred_element_type=jnp.float32
            ).astype(jnp.bfloat16)
            dv_copy(s).start()

    dv_acc[...] = jnp.dot(expo[j], cots[...], preferred_element_type=jnp.float32)

    group_wait(3)

    @pl.loop(0, BANDS)
    def _(i):
        first = pl.multiple_of(i * 256, 256)
        x_t[pl.ds(first, 256), :] = jnp.transpose(x_g[:, pl.ds(first, 256)])

    def pick_copy(s):
        peer = (me + s) % MEMBERS
        return pltpu.make_async_remote_copy(
            src_ref=picked.at[s],
            dst_ref=place(source, me),
            send_sem=pick_send.at[s],
            recv_sem=pick_recv.at[s],
            device_id={"member": peer},
            device_id_type=MESH,
        )

    @pl.when(sorts)
    def _():
        @pl.loop(1, MEMBERS)
        def _(s):
            pltpu.make_async_remote_copy(
                src_ref=picked.at[s],
                dst_ref=dealt.at[(me + MEMBERS - s) % MEMBERS],
                send_sem=deal_send.at[s],
                recv_sem=deal_recv.at[s],
                device_id={"member": (me + s) % MEMBERS},
                device_id_type=MESH,
            ).wait_recv()

        @pl.loop(1, MEMBERS)
        def _(s):
            picked[s] = dealt[winners[(me + s) % MEMBERS]]
            pick_copy(s).start()

        source[me // 8, pl.ds(me % 8 * PIECE, PIECE)] = dealt[winners[me]]

    for s in range(1, 4):

        @pl.when(j + s < 4)
        def _(s=s):
            dv_copy(s).wait_recv()
            dv_acc[...] += dv_in[s].astype(jnp.float32)

    def gr_copy(s):
        return pltpu.make_async_remote_copy(
            src_ref=gr_out.at[s],
            dst_ref=gr_in.at[s],
            send_sem=gr_send.at[s],
            recv_sem=gr_recv.at[s],
            device_id={"fsdp": (j + s) % 4 * 4 + g},
            device_id_type=MESH,
        )

    dv_low = dv_acc[...].astype(jnp.bfloat16)

    def rows_of(quarter):
        first = pl.multiple_of(quarter * 4 * ROWS, 16)
        return jnp.dot(
            x_t[pl.ds(first, 4 * ROWS), :], dv_low, preferred_element_type=jnp.float32
        )

    for s in range(1, 4):
        gr_out[s] = rows_of((j + s) % 4).astype(jnp.bfloat16)
        gr_copy(s).start()
    gr_acc[...] = rows_of(j)
    for s in range(1, 4):
        gr_copy(s).wait_recv()
        gr_acc[...] += gr_in[s].astype(jnp.float32)
    sum_out[...] = gr_acc[...].astype(jnp.bfloat16)

    def own_copy(s):
        peer = (g + s) % 4
        return pltpu.make_async_remote_copy(
            src_ref=sum_out.at[pl.ds(peer * ROWS, ROWS)],
            dst_ref=grad.at[g],
            send_sem=own_send.at[s],
            recv_sem=own_recv.at[s],
            device_id={"fsdp": j * 4 + peer},
            device_id_type=MESH,
        )

    for s in range(1, 4):
        own_copy(s).start()
    grad[g] = sum_out[pl.ds(pl.multiple_of(g * ROWS, 16), ROWS), :]
    for s in range(1, 4):
        slot = grad.at[(g + 4 - s) % 4]
        pltpu.make_async_remote_copy(
            src_ref=slot,
            dst_ref=slot,
            send_sem=own_send.at[s],
            recv_sem=own_recv.at[s],
            device_id={"fsdp": j * 4 + (g + s) % 4},
            device_id_type=MESH,
        ).wait_recv()

    @pl.loop(1, MEMBERS)
    def _(s):
        peer = (me + MEMBERS - s) % MEMBERS

        @pl.when(peer % 8 != BANDS)
        def _():
            slot = place(source, peer)
            pltpu.make_async_remote_copy(
                src_ref=slot,
                dst_ref=slot,
                send_sem=pick_send.at[s],
                recv_sem=pick_recv.at[s],
                device_id={"member": (me + s) % MEMBERS},
                device_id_type=MESH,
            ).wait_recv()

    for band in range(4):
        cols = slice(band * 256, (band + 1) * 256)
        gradient = grad[band].astype(jnp.float32)
        old_w = source[band, 0:ROWS].astype(jnp.float32)
        old_m = source[band, ROWS : 2 * ROWS].astype(jnp.float32)
        old_v = source[band, 2 * ROWS : 3 * ROWS].astype(jnp.float32)
        first = beta_one * old_m + (1.0 - beta_one) * gradient
        second = beta_two * old_v + (1.0 - beta_two) * gradient * gradient
        first_hat = first * (1.0 / (1.0 - beta_one**adam_step))
        second_hat = second * (1.0 / (1.0 - beta_two**adam_step))
        update = first_hat / (jnp.sqrt(second_hat) + adam_eps) + decay_rate * old_w
        new_w[:, cols] = (old_w - learning_rate * update).astype(jnp.bfloat16)
        new_m[:, cols] = first
        new_v[:, cols] = second

    for kind in range(4):
        for s in range(1, 4):
            group_copy(kind, s).wait_send()
    for s in range(1, 4):

        @pl.when(j + s < 4)
        def _(s=s):
            key_copy(s).wait_send()

        @pl.when(j >= s)
        def _(s=s):
            dv_copy(s).wait_send()

        gr_copy(s).wait_send()
        own_copy(s).wait_send()

    @pl.loop(1, MEMBERS)
    def _(s):
        @pl.when((me + s) % 8 != BANDS)
        def _():
            deal_copy(s).wait_send()

        @pl.when(sorts)
        def _():
            pick_copy(s).wait_send()


def local(inputs, queries, keys, cotangent, winners, weights, first_moment, second_moment):
    f32, bf16 = jnp.float32, jnp.bfloat16
    vmem = pl.BlockSpec(memory_space=pltpu.VMEM)
    hbm = pl.BlockSpec(memory_space=pl.ANY)
    dma = pltpu.SemaphoreType.DMA
    outs = pl.pallas_call(
        kernel,
        out_shape=(
            jax.ShapeDtypeStruct((ROWS, KVW), bf16),
            jax.ShapeDtypeStruct((ROWS, KVW), f32),
            jax.ShapeDtypeStruct((ROWS, KVW), f32),
        ),
        in_specs=[pl.BlockSpec(memory_space=pltpu.SMEM), hbm, hbm, hbm, hbm, vmem, vmem, vmem],
        out_specs=(vmem, vmem, vmem),
        scratch_shapes=[
            pltpu.VMEM((QUARTERS, PART, HEAD_DIM), bf16),
            pltpu.VMEM((PART, GROUP_HEADS * HEAD_DIM), bf16),
            pltpu.VMEM((PART, GROUP_HEADS * HEAD_DIM), bf16),
            pltpu.VMEM((PART, FEAT), bf16),
            pltpu.VMEM((FEAT, PART), bf16),
            pltpu.VMEM((QUARTERS, PART, GROUP_HEADS * PART), bf16),
            pltpu.VMEM((1, GROUP_HEADS * PART), f32),
            pltpu.VMEM((GROUP_HEADS * PART, HEAD_DIM), bf16),
            pltpu.VMEM((PART, HEAD_DIM), f32),
            pltpu.VMEM((4, PART, HEAD_DIM), bf16),
            pltpu.VMEM((4, PART, HEAD_DIM), bf16),
            pltpu.VMEM((4 * ROWS, HEAD_DIM), f32),
            pltpu.VMEM((4, 4 * ROWS, HEAD_DIM), bf16),
            pltpu.VMEM((4, 4 * ROWS, HEAD_DIM), bf16),
            pltpu.VMEM((4 * ROWS, HEAD_DIM), bf16),
            pltpu.VMEM((4, ROWS, HEAD_DIM), bf16),
            pltpu.VMEM((4, 3 * ROWS, 256), bf16),
            pltpu.VMEM((MEMBERS, PIECE, 256), bf16),
            pltpu.VMEM((MEMBERS, PIECE, 256), bf16),
            pltpu.VMEM((4, 3 * ROWS, 256), bf16),
            dma((4,)),
            dma((4, 4)),
            dma((4, 4)),
            dma((4,)),
            dma((4,)),
            dma((4,)),
            dma((4,)),
            dma((4,)),
            dma((4,)),
            dma((4,)),
            dma((4,)),
            dma((MEMBERS,)),
            dma((MEMBERS,)),
            dma((MEMBERS,)),
            dma((MEMBERS,)),
        ],
        compiler_params=pltpu.CompilerParams(
            collective_id=0, has_side_effects=True, vmem_limit_bytes=48 * 1024 * 1024
        ),
        cost_estimate=pl.CostEstimate(
            flops=3_000_000_000, bytes_accessed=6_000_000, transcendentals=4_000_000
        ),
    )(
        winners, inputs[0], queries[0], keys[0], cotangent[0],
        weights[0], first_moment[0], second_moment[0],
    )
    return tuple(out[None] for out in outs)


def solution(mesh):
    rows = P("member", "fsdp", None)
    return jax.shard_map(
        local,
        mesh=mesh,
        in_specs=(rows, rows, rows, rows, P(), rows, rows, rows),
        out_specs=(rows, rows, rows),
        check_vma=False,
    )
```

time: 352 us -> 105 us (0.30); the launches traced: 345 us -> 104 us
  waiting for transfers between devices: 216 us -> 0 us
  Pallas kernels: 0 us -> 93.3 us
  starting transfers between devices: 48.7 us -> 0 us
  matrix products: 24.5 us -> 0 us
  other arithmetic: 17.4 us -> 0 us
  local copies, waits for them, and re-layouts: 24.6 us -> 9.9 us
  between operations: 14 us -> 0.66 us
    all_gather x2 -> x0, waiting for transfers between devices: 143 us -> none  [the longest x1 85.2 us: local(): x_piece = lax.all_gather(x_rows, 'fsdp', axis=0, tiled=True)]
    pallas_call x0 -> x1, Pallas kernels: none -> 93.3 us  [local(): pl.pallas_call(kernel, out_shape=(jax.ShapeDtypeStruct((ROWS, KVW), bf16)...]
    all_to_all x6 -> x0, waiting for transfers between devices: 72 us -> none  [the longest x1 16 us: local(): lax.all_to_all(second_moment.reshape(1, -1).astype(jnp.bfloat16), 'member...]
    all_to_all x6 -> x0, starting transfers between devices: 48.5 us -> none  [the longest x1 16.2 us: local(): lax.all_to_all(first_moment.reshape(1, -1).astype(jnp.bfloat16), 'member'...]
    dot_general x3 -> x0, matrix products: 24.5 us -> none  [the longest x1 13.7 us: compute(): jnp.einsum('kgrn,nc->kgrc', weights_exp.astype(jnp.bfloat16), x_piece, pr...]
    reshape x1 -> x0, local copies, waits for them, and re-layouts: 7.86 us -> none  [compute(): key_heads = k_piece.reshape(key_count, KV_HEADS, HEAD_DIM)]
    convert_element_type x4 -> x0, local copies, waits for them, and re-layouts: 6.5 us -> none  [the longest x1 6.04 us: local(): term.reshape(lax.axis_size('fsdp') * (feat_width // fsdp_size), kv_width)]
    unnamed x3 -> x0, other arithmetic: 5.95 us -> none
  transfers between devices with their start and end apart: 9 -> 0, of which waited for: 7 -> 0; matrix products, arithmetic and copies ran while one was open for 19% -> 0% of each run, Pallas kernels for 0% -> 0%
where the time goes in v1:
time: 105 us; the launch traced here: 104 us
  Pallas kernels  93.3 us (89%)
  local copies, waits for them, and re-layouts  9.9 us (9%)
    pallas_call x1, Pallas kernels, local(): pl.pallas_call(kernel, out_shape=(jax.ShapeDtypeStruct((ROWS, KVW), bf16)...  93.3 us
    unnamed x19, local copies, waits for them, and re-layouts  9.9 us

profile of v1, /device:TPU:7, one launch (start us, length us, event | category | flops | bytes accessed | tf_op | source)
XLA Modules:
  0.0 103.8 jit_solution(7333986834157660577)
XLA Ops:
  0.6 0.0 copy-start.7
  0.6 0.6 copy-done.7
  1.3 0.0 copy-start
  1.3 1.0 %copy-done = bf16[1,128,2048]{2,1,0:T(8,128)(2,1)S(1)} copy-done((bf16[1,128,2048]{2,1,0:T(8,128)(2,1)S(1)}, bf16[1,128,2048]{2,1,0:T(8,128)(2,1)}, u32[]{:S(2)}) %copy-start) | copy-done | bytes 524312
  2.3 0.0 copy-start.1
  2.3 1.0 %copy-done.1 = bf16[1,128,2048]{2,1,0:T(8,128)(2,1)S(1)} copy-done((bf16[1,128,2048]{2,1,0:T(8,128)(2,1)S(1)}, bf16[1,128,2048]{2,1,0:T(8,128)(2,1)}, u32[]{:S(2)}) %copy-start.1) | copy-done | bytes 524312
  3.4 0.0 copy-start.2
  3.4 1.0 copy-done.2
  4.4 0.0 copy-start.3
  4.4 1.0 copy-done.3
  5.4 0.0 copy-start.4
  5.4 1.0 copy-done.4
  6.4 0.0 copy-start.5
  6.4 0.9 copy-done.5
  7.4 0.0 copy-start.6
  7.4 0.9 copy-done.6
  8.3 93.3 %shard_map.103 = (bf16[112,1024]{1,0:T(8,128)(2,1)S(1)}, f32[112,1024]{1,0:T(8,128)S(1)}, f32[112,1024]{1,0:T(8,128)S(1)}) custom-call(s32[32]{0:T(128)S(1)} %copy-done.7, bf16[128,1792]{1,0:T(8,128)(2,1)S(1)} %bitcast.15, bf16[128,2048]{1,0:T(8,128)(2,1)S(1)} %bitcast.13, bf16[128,1024]{1,0:T(8,128)(2,1)S(1)} %bitcast.18, bf16[128,2048]{1,0:T(8,128)(2,1)S(1)} %bitcast.14, ...), custom_call_target="tpu_custom_call" | custom-call | flops 3000000000 | bytes 6000000 | tf_op jit(solution)/shard_map/pallas_call | solution.py:394
  101.6 0.7 copy.14
  102.3 0.8 copy.15
  103.1 0.8 copy.16
Async XLA Ops:
  0.6 0.7 copy-start.7
  1.3 1.0 %copy-start = (bf16[1,128,2048]{2,1,0:T(8,128)(2,1)S(1)}, bf16[1,128,2048]{2,1,0:T(8,128)(2,1)}, u32[]{:S(2)}) copy-start(bf16[1,128,2048]{2,1,0:T(8,128)(2,1)} %param.9) | copy-start | bytes 1572868
  2.3 1.0 %copy-start.1 = (bf16[1,128,2048]{2,1,0:T(8,128)(2,1)S(1)}, bf16[1,128,2048]{2,1,0:T(8,128)(2,1)}, u32[]{:S(2)}) copy-start(bf16[1,128,2048]{2,1,0:T(8,128)(2,1)} %param.11) | copy-start | bytes 1572868
  3.4 1.0 copy-start.2
  4.4 1.0 copy-start.3
  5.4 1.0 copy-start.4
  6.4 0.9 copy-start.5
  7.4 0.9 copy-start.6

commit v2 on v1

--- a/solution.py
+++ b/solution.py
@@ -15,8 +15,8 @@
 ROWS = 112
 KVW = 1024
 PART = QUARTERS * TOK
-PIECE = 48
-BANDS = 7
+PIECE = 80
+BLOCKS = 7
 
 beta_one = 0.9
 beta_two = 0.999
@@ -26,22 +26,31 @@
 adam_step = 200
 soft_cap = 50.0
 
+VMEM_LIMIT = 60 * 1024 * 1024
+
 MESH = pl.DeviceIdType.MESH
 
 
 def kernel(
     winners, x_in, q_in, k_in, c_in, w_in, m_in, v_in,
-    new_w, new_m, new_v,
+    grad_out, source_out,
     k_all, q_g, c_g, x_g, x_t, expo, denom, cots,
     dv_acc, dv_out, dv_in, gr_acc, gr_out, gr_in, sum_out, grad,
-    state, dealt, picked, source,
-    loc_sem, grp_send, grp_recv, key_send, key_recv, dv_send, dv_recv,
-    gr_send, gr_recv, own_send, own_recv, deal_send, deal_recv, pick_send, pick_recv,
+    w_own, m_own, v_own, state, dealt_0, dealt_1, dealt_2, picked_0, picked_1, picked_2, source,
+    loc_sem, own_sem, out_sem, grp_send, grp_recv, key_send, key_recv, dv_send, dv_recv,
+    gr_send, gr_recv, own_send, own_recv, fwd_send, fwd_recv, deal_send, deal_recv, pick_send, pick_recv,
 ):
     me = lax.axis_index("member")
     mine = lax.axis_index("fsdp")
     j = mine // KV_HEADS
     g = mine % KV_HEADS
+
+    state_copies = [
+        pltpu.make_async_copy(src, dst, own_sem.at[i])
+        for i, (src, dst) in enumerate(((w_in, w_own), (m_in, m_own), (v_in, v_own)))
+    ]
+    for copy in state_copies:
+        copy.start()
 
     barrier = pltpu.get_barrier_semaphore()
     for s in range(1, 4):
@@ -100,11 +109,13 @@
     for kind in range(4):
         local_copy(kind).start()
 
-    for band in range(4):
-        cols = slice(band * 256, (band + 1) * 256)
-        state[band, 0:ROWS] = w_in[:, cols]
-        state[band, ROWS : 2 * ROWS] = m_in[:, cols].astype(jnp.bfloat16)
-        state[band, 2 * ROWS : 3 * ROWS] = v_in[:, cols].astype(jnp.bfloat16)
+    for copy in state_copies:
+        copy.wait()
+    for band in range(8):
+        cols = slice(band * 128, (band + 1) * 128)
+        state[band, 0:ROWS] = w_own[:, cols]
+        state[band, ROWS : 2 * ROWS] = m_own[:, cols].astype(jnp.bfloat16)
+        state[band, 2 * ROWS : 3 * ROWS] = v_own[:, cols].astype(jnp.bfloat16)
 
     pl.semaphore_wait(barrier, 6 + MEMBERS - 1)
 
@@ -112,34 +123,114 @@
         for s in range(1, 4):
             group_copy(kind, s).start()
 
-    sorts = me % 8 != BANDS
-
-    def place(ref, member):
-        return ref.at[member // 8, pl.ds(member % 8 * PIECE, PIECE)]
-
-    def deal_copy(s):
+    sibling = g + 1 - 2 * (g % 2)
+
+    def x_copy(owner, peer, sem):
+        slot = own_slot(3, owner)
+        return pltpu.make_async_remote_copy(
+            src_ref=x_in if sem < 2 else slot,
+            dst_ref=slot,
+            send_sem=fwd_send.at[sem],
+            recv_sem=fwd_recv.at[sem],
+            device_id={"fsdp": j * 4 + peer},
+            device_id_type=MESH,
+        )
+
+    def x_wait(owner, sem):
+        slot = own_slot(3, owner)
+        pltpu.make_async_remote_copy(
+            src_ref=slot,
+            dst_ref=slot,
+            send_sem=fwd_send.at[sem],
+            recv_sem=fwd_recv.at[sem],
+            device_id={"fsdp": j * 4 + sibling},
+            device_id_type=MESH,
+        ).wait_recv()
+
+    core = mine % 2
+    starts, sizes = (0, 48, 80), (48, 32, 16)
+    dealt, picked = (dealt_0, dealt_1, dealt_2), (picked_0, picked_1, picked_2)
+
+    def extra(member):
+        return (member + 2 * core) % 4 == 1
+
+    def sorts(member, part, action):
+        if part < 2:
+            action()
+        else:
+            pl.when(extra(member))(action)
+
+    def place(ref, member, part):
+        first = member % 4 * PIECE + starts[part] if part < 2 else 4 * PIECE
+        return ref.at[member // 4, pl.ds(first, sizes[part])]
+
+    def deal_copy(s, part):
         peer = (me + s) % MEMBERS
         return pltpu.make_async_remote_copy(
-            src_ref=place(state, peer),
-            dst_ref=dealt.at[me],
-            send_sem=deal_send.at[s],
-            recv_sem=deal_recv.at[s],
+            src_ref=place(state, peer, part),
+            dst_ref=dealt[part].at[me],
+            send_sem=deal_send.at[part],
+            recv_sem=deal_recv.at[part],
             device_id={"member": peer},
             device_id_type=MESH,
         )
 
-    @pl.loop(1, MEMBERS)
-    def _(s):
-        @pl.when((me + s) % 8 != BANDS)
-        def _():
-            deal_copy(s).start()
-
-    for s in range(1, 4):
-        group_copy(3, s).start()
-
-    @pl.when(sorts)
-    def _():
-        dealt[me] = state[me // 8, pl.ds(me % 8 * PIECE, PIECE)]
+    def all_of(part, count, send_sem, recv_sem):
+        ref = dealt[part].at[pl.ds(0, count)]
+        return pltpu.make_async_remote_copy(
+            src_ref=ref,
+            dst_ref=ref,
+            send_sem=send_sem.at[part],
+            recv_sem=recv_sem.at[part],
+            device_id={"member": (me + 1) % MEMBERS},
+            device_id_type=MESH,
+        )
+
+    def to_or_from_sorters(part, wait):
+        if part < 2:
+            wait(MEMBERS - 1)
+        else:
+            pl.when(extra(me))(lambda: wait(MEMBERS // 4 - 1))
+            pl.when(jnp.logical_not(extra(me)))(lambda: wait(MEMBERS // 4))
+
+    for part in range(3):
+
+        @pl.loop(1, MEMBERS)
+        def _(s):
+            sorts((me + s) % MEMBERS, part, lambda: deal_copy(s, part).start())
+
+    x_copy(g, sibling, 0).start()
+    x_copy(g, (g + 2) % 4, 1).start()
+
+    def keep(part):
+        dealt[part][me] = place(state, me, part)[...]
+
+    for part in range(3):
+        sorts(me, part, lambda: keep(part))
+
+    def pick_copy(s, part):
+        peer = (me + s) % MEMBERS
+        return pltpu.make_async_remote_copy(
+            src_ref=picked[part].at[s],
+            dst_ref=place(source, me, part),
+            send_sem=pick_send.at[part],
+            recv_sem=pick_recv.at[part],
+            device_id={"member": peer},
+            device_id_type=MESH,
+        )
+
+    def pick(part):
+        def action():
+            all_of(part, MEMBERS - 1, deal_send, deal_recv).wait_recv()
+
+            @pl.loop(1, MEMBERS)
+            def _(s):
+                picked[part][s] = dealt[part][winners[(me + s) % MEMBERS]]
+                pick_copy(s, part).start()
+
+            place(source, me, part)[...] = dealt[part][winners[me]]
+
+        sorts(me, part, action)
 
     def key_copy(s):
         return pltpu.make_async_remote_copy(
@@ -231,43 +322,19 @@
 
     dv_acc[...] = jnp.dot(expo[j], cots[...], preferred_element_type=jnp.float32)
 
-    group_wait(3)
-
-    @pl.loop(0, BANDS)
+    x_wait((g + 2) % 4, 1)
+    x_copy((g + 2) % 4, sibling, 2).start()
+
+    pick(0)
+
+    x_wait(sibling, 0)
+    x_wait((sibling + 2) % 4, 2)
+    local_copy(3).wait()
+
+    @pl.loop(0, BLOCKS)
     def _(i):
         first = pl.multiple_of(i * 256, 256)
         x_t[pl.ds(first, 256), :] = jnp.transpose(x_g[:, pl.ds(first, 256)])
-
-    def pick_copy(s):
-        peer = (me + s) % MEMBERS
-        return pltpu.make_async_remote_copy(
-            src_ref=picked.at[s],
-            dst_ref=place(source, me),
-            send_sem=pick_send.at[s],
-            recv_sem=pick_recv.at[s],
-            device_id={"member": peer},
-            device_id_type=MESH,
-        )
-
-    @pl.when(sorts)
-    def _():
-        @pl.loop(1, MEMBERS)
-        def _(s):
-            pltpu.make_async_remote_copy(
-                src_ref=picked.at[s],
-                dst_ref=dealt.at[(me + MEMBERS - s) % MEMBERS],
-                send_sem=deal_send.at[s],
-                recv_sem=deal_recv.at[s],
-                device_id={"member": (me + s) % MEMBERS},
-                device_id_type=MESH,
-            ).wait_recv()
-
-        @pl.loop(1, MEMBERS)
-        def _(s):
-            picked[s] = dealt[winners[(me + s) % MEMBERS]]
-            pick_copy(s).start()
-
-        source[me // 8, pl.ds(me % 8 * PIECE, PIECE)] = dealt[winners[me]]
 
     for s in range(1, 4):
 
@@ -298,6 +365,10 @@
         gr_out[s] = rows_of((j + s) % 4).astype(jnp.bfloat16)
         gr_copy(s).start()
     gr_acc[...] = rows_of(j)
+
+    pick(1)
+    pick(2)
+
     for s in range(1, 4):
         gr_copy(s).wait_recv()
         gr_acc[...] += gr_in[s].astype(jnp.float32)
@@ -328,25 +399,53 @@
             device_id_type=MESH,
         ).wait_recv()
 
-    @pl.loop(1, MEMBERS)
-    def _(s):
-        peer = (me + MEMBERS - s) % MEMBERS
-
-        @pl.when(peer % 8 != BANDS)
-        def _():
-            slot = place(source, peer)
-            pltpu.make_async_remote_copy(
-                src_ref=slot,
-                dst_ref=slot,
-                send_sem=pick_send.at[s],
-                recv_sem=pick_recv.at[s],
-                device_id={"member": (me + s) % MEMBERS},
-                device_id_type=MESH,
-            ).wait_recv()
-
-    for band in range(4):
-        cols = slice(band * 256, (band + 1) * 256)
-        gradient = grad[band].astype(jnp.float32)
+    grad_copy = pltpu.make_async_copy(grad, grad_out, out_sem.at[0])
+    grad_copy.start()
+
+    for part in range(3):
+        to_or_from_sorters(
+            part, lambda count: all_of(part, count, deal_send, deal_recv).wait_send()
+        )
+    for part in range(3):
+        to_or_from_sorters(
+            part, lambda count: all_of(part, count, pick_send, pick_recv).wait_recv()
+        )
+
+    source_copy = pltpu.make_async_copy(source, source_out, out_sem.at[1])
+    source_copy.start()
+
+    for s in range(1, 4):
+        for kind in range(3):
+            group_copy(kind, s).wait_send()
+
+        @pl.when(j + s < 4)
+        def _(s=s):
+            key_copy(s).wait_send()
+
+        @pl.when(j >= s)
+        def _(s=s):
+            dv_copy(s).wait_send()
+
+        gr_copy(s).wait_send()
+        own_copy(s).wait_send()
+    x_copy(g, sibling, 0).wait_send()
+    x_copy(g, (g + 2) % 4, 1).wait_send()
+    x_copy((g + 2) % 4, sibling, 2).wait_send()
+
+    for part in range(3):
+        sorts(
+            me, part, lambda: all_of(part, MEMBERS - 1, pick_send, pick_recv).wait_send()
+        )
+
+    grad_copy.wait()
+    source_copy.wait()
+
+
+def adam_kernel(grad, source, new_w, new_m, new_v):
+    for band in range(8):
+        cols = slice(band * 128, (band + 1) * 128)
+        lanes = slice(band % 2 * 128, band % 2 * 128 + 128)
+        gradient = grad[band // 2, :, lanes].astype(jnp.float32)
         old_w = source[band, 0:ROWS].astype(jnp.float32)
         old_m = source[band, ROWS : 2 * ROWS].astype(jnp.float32)
         old_v = source[band, 2 * ROWS : 3 * ROWS].astype(jnp.float32)
@@ -359,47 +458,20 @@
         new_m[:, cols] = first
         new_v[:, cols] = second
 
-    for kind in range(4):
-        for s in range(1, 4):
-            group_copy(kind, s).wait_send()
-    for s in range(1, 4):
-
-        @pl.when(j + s < 4)
-        def _(s=s):
-            key_copy(s).wait_send()
-
-        @pl.when(j >= s)
-        def _(s=s):
-            dv_copy(s).wait_send()
-
-        gr_copy(s).wait_send()
-        own_copy(s).wait_send()
-
-    @pl.loop(1, MEMBERS)
-    def _(s):
-        @pl.when((me + s) % 8 != BANDS)
-        def _():
-            deal_copy(s).wait_send()
-
-        @pl.when(sorts)
-        def _():
-            pick_copy(s).wait_send()
-
 
 def local(inputs, queries, keys, cotangent, winners, weights, first_moment, second_moment):
     f32, bf16 = jnp.float32, jnp.bfloat16
     vmem = pl.BlockSpec(memory_space=pltpu.VMEM)
-    hbm = pl.BlockSpec(memory_space=pl.ANY)
+    hbm = pl.BlockSpec(memory_space=pltpu.HBM)
     dma = pltpu.SemaphoreType.DMA
-    outs = pl.pallas_call(
+    grad, source = pl.pallas_call(
         kernel,
         out_shape=(
-            jax.ShapeDtypeStruct((ROWS, KVW), bf16),
-            jax.ShapeDtypeStruct((ROWS, KVW), f32),
-            jax.ShapeDtypeStruct((ROWS, KVW), f32),
+            jax.ShapeDtypeStruct((4, ROWS, HEAD_DIM), bf16),
+            jax.ShapeDtypeStruct((8, 3 * ROWS, 128), bf16),
         ),
-        in_specs=[pl.BlockSpec(memory_space=pltpu.SMEM), hbm, hbm, hbm, hbm, vmem, vmem, vmem],
-        out_specs=(vmem, vmem, vmem),
+        in_specs=[pl.BlockSpec(memory_space=pltpu.SMEM)] + [hbm] * 7,
+        out_specs=(hbm, hbm),
         scratch_shapes=[
             pltpu.VMEM((QUARTERS, PART, HEAD_DIM), bf16),
             pltpu.VMEM((PART, GROUP_HEADS * HEAD_DIM), bf16),
@@ -417,11 +489,20 @@
             pltpu.VMEM((4, 4 * ROWS, HEAD_DIM), bf16),
             pltpu.VMEM((4 * ROWS, HEAD_DIM), bf16),
             pltpu.VMEM((4, ROWS, HEAD_DIM), bf16),
-            pltpu.VMEM((4, 3 * ROWS, 256), bf16),
-            pltpu.VMEM((MEMBERS, PIECE, 256), bf16),
-            pltpu.VMEM((MEMBERS, PIECE, 256), bf16),
-            pltpu.VMEM((4, 3 * ROWS, 256), bf16),
-            dma((4,)),
+            pltpu.VMEM((ROWS, KVW), bf16),
+            pltpu.VMEM((ROWS, KVW), f32),
+            pltpu.VMEM((ROWS, KVW), f32),
+            pltpu.VMEM((8, 3 * ROWS, 128), bf16),
+            pltpu.VMEM((MEMBERS, 48, 128), bf16),
+            pltpu.VMEM((MEMBERS, 32, 128), bf16),
+            pltpu.VMEM((MEMBERS, 16, 128), bf16),
+            pltpu.VMEM((MEMBERS, 48, 128), bf16),
+            pltpu.VMEM((MEMBERS, 32, 128), bf16),
+            pltpu.VMEM((MEMBERS, 16, 128), bf16),
+            pltpu.VMEM((8, 3 * ROWS, 128), bf16),
+            dma((4,)),
+            dma((3,)),
+            dma((2,)),
             dma((4, 4)),
             dma((4, 4)),
             dma((4,)),
@@ -432,13 +513,15 @@
             dma((4,)),
             dma((4,)),
             dma((4,)),
-            dma((MEMBERS,)),
-            dma((MEMBERS,)),
-            dma((MEMBERS,)),
-            dma((MEMBERS,)),
+            dma((4,)),
+            dma((4,)),
+            dma((3,)),
+            dma((3,)),
+            dma((3,)),
+            dma((3,)),
         ],
         compiler_params=pltpu.CompilerParams(
-            collective_id=0, has_side_effects=True, vmem_limit_bytes=48 * 1024 * 1024
+            collective_id=0, has_side_effects=True, vmem_limit_bytes=VMEM_LIMIT
         ),
         cost_estimate=pl.CostEstimate(
             flops=3_000_000_000, bytes_accessed=6_000_000, transcendentals=4_000_000
@@ -447,6 +530,17 @@
         winners, inputs[0], queries[0], keys[0], cotangent[0],
         weights[0], first_moment[0], second_moment[0],
     )
+    outs = pl.pallas_call(
+        adam_kernel,
+        out_shape=(
+            jax.ShapeDtypeStruct((ROWS, KVW), bf16),
+            jax.ShapeDtypeStruct((ROWS, KVW), f32),
+            jax.ShapeDtypeStruct((ROWS, KVW), f32),
+        ),
+        in_specs=[vmem, vmem],
+        out_specs=(vmem, vmem, vmem),
+        compiler_params=pltpu.CompilerParams(vmem_limit_bytes=VMEM_LIMIT),
+    )(grad, source)
     return tuple(out[None] for out in outs)
 
 

time: 105 us -> 89.4 us (0.85)
  local copies, waits for them, and re-layouts: 9.9 us -> 0 us
  Pallas kernels: 93.3 us -> 87.7 us
    unnamed x19 -> x0, local copies, waits for them, and re-layouts: 9.9 us -> none
    pallas_call x1 -> x2, Pallas kernels: 93.3 us -> 87.7 us  [the longest x1 85.1 us: local(): pl.pallas_call(kernel, out_shape=(jax.ShapeDtypeStruct((4, ROWS, HEAD_DIM...]
where the time goes in v2:
time: 89.4 us; the launch traced here: 88.3 us
  Pallas kernels  87.7 us (98%)
    pallas_call x1, Pallas kernels, local(): pl.pallas_call(kernel, out_shape=(jax.ShapeDtypeStruct((4, ROWS, HEAD_DIM...  85.1 us
    pallas_call x1, Pallas kernels, local(): pl.pallas_call(adam_kernel, out_shape=(jax.ShapeDtypeStruct((ROWS, KVW),...  2.56 us

profile of v2, /device:TPU:7, one launch (start us, length us, event | category | flops | bytes accessed | tf_op | source)
XLA Modules:
  0.0 88.3 jit_solution(16894751408517628101)
XLA Ops:
  0.6 85.1 %shard_map.103 = (bf16[4,112,256]{2,1,0:T(8,128)(2,1)}, bf16[8,336,128]{2,1,0:T(8,128)(2,1)}) custom-call(s32[32]{0:T(128)} %winners.1, bf16[128,1792]{1,0:T(8,128)(2,1)} %bitcast.12, bf16[128,2048]{1,0:T(8,128)(2,1)} %bitcast.10, bf16[128,1024]{1,0:T(8,128)(2,1)} %bitcast.17, bf16[128,2048]{1,0:T(8,128)(2,1)} %bitcast.11, bf16[112,1024]{1,0:T(8,128)(2,1)} %bitcast.18, ...), custom_call_target="tpu_custom_call" | custom-call | flops 3000000000 | bytes 6000000 | tf_op jit(solution)/shard_map/pallas_call | solution.py:467
  85.8 2.6 %shard_map.104 = (bf16[112,1024]{1,0:T(8,128)(2,1)}, f32[112,1024]{1,0:T(8,128)}, f32[112,1024]{1,0:T(8,128)}) custom-call(bf16[4,112,256]{2,1,0:T(8,128)(2,1)} %get-tuple-element.8.grad, bf16[8,336,128]{2,1,0:T(8,128)(2,1)} %get-tuple-element.9.source), custom_call_target="tpu_custom_call" | custom-call | tf_op jit(solution)/shard_map/pallas_call | solution.py:533

commit v3 on v2

--- a/solution.py
+++ b/solution.py
@@ -38,12 +38,15 @@
     dv_acc, dv_out, dv_in, gr_acc, gr_out, gr_in, sum_out, grad,
     w_own, m_own, v_own, state, dealt_0, dealt_1, dealt_2, picked_0, picked_1, picked_2, source,
     loc_sem, own_sem, out_sem, grp_send, grp_recv, key_send, key_recv, dv_send, dv_recv,
-    gr_send, gr_recv, own_send, own_recv, fwd_send, fwd_recv, deal_send, deal_recv, pick_send, pick_recv,
+    gr_send, gr_recv, own_send, own_recv, deal_send, deal_recv, pick_send, pick_recv,
 ):
     me = lax.axis_index("member")
     mine = lax.axis_index("fsdp")
-    j = mine // KV_HEADS
-    g = mine % KV_HEADS
+    g = mine // QUARTERS
+    j = mine % QUARTERS
+
+    def at(quarter, head):
+        return {"fsdp": head * QUARTERS + quarter}
 
     state_copies = [
         pltpu.make_async_copy(src, dst, own_sem.at[i])
@@ -55,10 +58,10 @@
     barrier = pltpu.get_barrier_semaphore()
     for s in range(1, 4):
         pl.semaphore_signal(
-            barrier, inc=1, device_id={"fsdp": j * 4 + (g + s) % 4}, device_id_type=MESH
+            barrier, inc=1, device_id=at(j, (g + s) % 4), device_id_type=MESH
         )
         pl.semaphore_signal(
-            barrier, inc=1, device_id={"fsdp": (j + s) % 4 * 4 + g}, device_id_type=MESH
+            barrier, inc=1, device_id=at((j + s) % 4, g), device_id_type=MESH
         )
 
     @pl.loop(1, MEMBERS)
@@ -86,7 +89,7 @@
             dst_ref=own_slot(kind, g),
             send_sem=grp_send.at[kind, s],
             recv_sem=grp_recv.at[kind, s],
-            device_id={"fsdp": j * 4 + peer},
+            device_id=at(j, peer),
             device_id_type=MESH,
         )
 
@@ -98,7 +101,7 @@
                 dst_ref=slot,
                 send_sem=grp_send.at[kind, s],
                 recv_sem=grp_recv.at[kind, s],
-                device_id={"fsdp": j * 4 + (g + s) % 4},
+                device_id=at(j, (g + s) % 4),
                 device_id_type=MESH,
             ).wait_recv()
         local_copy(kind).wait()
@@ -123,30 +126,6 @@
         for s in range(1, 4):
             group_copy(kind, s).start()
 
-    sibling = g + 1 - 2 * (g % 2)
-
-    def x_copy(owner, peer, sem):
-        slot = own_slot(3, owner)
-        return pltpu.make_async_remote_copy(
-            src_ref=x_in if sem < 2 else slot,
-            dst_ref=slot,
-            send_sem=fwd_send.at[sem],
-            recv_sem=fwd_recv.at[sem],
-            device_id={"fsdp": j * 4 + peer},
-            device_id_type=MESH,
-        )
-
-    def x_wait(owner, sem):
-        slot = own_slot(3, owner)
-        pltpu.make_async_remote_copy(
-            src_ref=slot,
-            dst_ref=slot,
-            send_sem=fwd_send.at[sem],
-            recv_sem=fwd_recv.at[sem],
-            device_id={"fsdp": j * 4 + sibling},
-            device_id_type=MESH,
-        ).wait_recv()
-
     core = mine % 2
     starts, sizes = (0, 48, 80), (48, 32, 16)
     dealt, picked = (dealt_0, dealt_1, dealt_2), (picked_0, picked_1, picked_2)
@@ -199,8 +178,8 @@
         def _(s):
             sorts((me + s) % MEMBERS, part, lambda: deal_copy(s, part).start())
 
-    x_copy(g, sibling, 0).start()
-    x_copy(g, (g + 2) % 4, 1).start()
+    for s in range(1, 4):
+        group_copy(3, s).start()
 
     def keep(part):
         dealt[part][me] = place(state, me, part)[...]
@@ -238,7 +217,7 @@
             dst_ref=k_all.at[j],
             send_sem=key_send.at[s],
             recv_sem=key_recv.at[s],
-            device_id={"fsdp": (j + s) % 4 * 4 + g},
+            device_id=at((j + s) % 4, g),
             device_id_type=MESH,
         )
 
@@ -249,48 +228,43 @@
             dst_ref=slot,
             send_sem=key_send.at[s],
             recv_sem=key_recv.at[s],
-            device_id={"fsdp": (j + s) % 4 * 4 + g},
+            device_id=at((j + s) % 4, g),
             device_id_type=MESH,
         ).wait_recv()
 
     group_wait(0)
     for s in range(1, 4):
-
-        @pl.when(j + s < 4)
-        def _(s=s):
-            key_copy(s).start()
+        key_copy(s).start()
 
     group_wait(1)
     denom[...] = jnp.zeros_like(denom)
 
-    def scores(chunk, diagonal):
-        @pl.loop(0, 4)
-        def _(block):
-            first = pl.multiple_of(block * TOK, TOK)
-            key_block = k_all[chunk, pl.ds(first, TOK), :]
+    def scores(chunk):
+        later = jnp.where(chunk > j, TOK, jnp.where(chunk < j, -TOK, 0))
+        for i in range(4):
+            first = i * TOK
+            key_block = k_all[chunk, first : first + TOK, :]
             for h in range(GROUP_HEADS):
                 raw = lax.dot_general(
                     key_block,
-                    q_g[:, h * HEAD_DIM : (h + 1) * HEAD_DIM],
+                    q_g[first:PART, h * HEAD_DIM : (h + 1) * HEAD_DIM],
                     (((1,), (1,)), ((), ())),
                     preferred_element_type=jnp.float32,
                 )
                 e = jnp.exp(soft_cap * jnp.tanh(raw * (HEAD_DIM**-0.5 / soft_cap)))
-                if diagonal:
-                    u = first + lax.broadcasted_iota(jnp.int32, (TOK, PART), 0)
-                    t = lax.broadcasted_iota(jnp.int32, (TOK, PART), 1)
-                    e = jnp.where(u <= t, e, 0.0)
-                cols = slice(h * PART, (h + 1) * PART)
-                expo[chunk, pl.ds(first, TOK), cols] = e.astype(jnp.bfloat16)
+                u = lax.broadcasted_iota(jnp.int32, raw.shape, 0)
+                t = lax.broadcasted_iota(jnp.int32, raw.shape, 1)
+                e = jnp.where((u + later <= t) | (t >= TOK), e, 0.0)
+                cols = slice(h * PART + first, (h + 1) * PART)
+                expo[chunk, first : first + TOK, cols] = e.astype(jnp.bfloat16)
                 denom[:, cols] += jnp.sum(e, axis=0, keepdims=True)
 
-    scores(j, True)
-    for s in range(1, 4):
-
-        @pl.when(j >= s)
-        def _(s=s):
-            key_wait(s)
-            scores(j - s, False)
+    scores(j)
+
+    @pl.loop(1, 4)
+    def _(s):
+        key_wait(s)
+        scores((j + 4 - s) % 4)
 
     group_wait(2)
     for h in range(GROUP_HEADS):
@@ -307,29 +281,35 @@
             dst_ref=dv_in.at[s],
             send_sem=dv_send.at[s],
             recv_sem=dv_recv.at[s],
-            device_id={"fsdp": (j + 4 - s) % 4 * 4 + g},
-            device_id_type=MESH,
-        )
-
-    for s in range(1, 4):
-
-        @pl.when(j >= s)
-        def _(s=s):
-            dv_out[s] = jnp.dot(
-                expo[j - s], cots[...], preferred_element_type=jnp.float32
-            ).astype(jnp.bfloat16)
-            dv_copy(s).start()
-
-    dv_acc[...] = jnp.dot(expo[j], cots[...], preferred_element_type=jnp.float32)
-
-    x_wait((g + 2) % 4, 1)
-    x_copy((g + 2) % 4, sibling, 2).start()
+            device_id=at((j + 4 - s) % 4, g),
+            device_id_type=MESH,
+        )
+
+    def dv_rows(chunk, i):
+        first = i * TOK
+        total = None
+        for h in range(GROUP_HEADS):
+            cols = slice(h * PART + first, (h + 1) * PART)
+            term = jnp.dot(
+                expo[chunk, first : first + TOK, cols],
+                cots[cols, :],
+                preferred_element_type=jnp.float32,
+            )
+            total = term if total is None else total + term
+        return total
+
+    @pl.loop(1, 4)
+    def _(s):
+        for i in range(4):
+            dv_out[s, i * TOK : (i + 1) * TOK] = dv_rows((j + 4 - s) % 4, i).astype(jnp.bfloat16)
+        dv_copy(s).start()
+
+    for i in range(4):
+        dv_acc[i * TOK : (i + 1) * TOK] = dv_rows(j, i)
 
     pick(0)
 
-    x_wait(sibling, 0)
-    x_wait((sibling + 2) % 4, 2)
-    local_copy(3).wait()
+    group_wait(3)
 
     @pl.loop(0, BLOCKS)
     def _(i):
@@ -337,11 +317,8 @@
         x_t[pl.ds(first, 256), :] = jnp.transpose(x_g[:, pl.ds(first, 256)])
 
     for s in range(1, 4):
-
-        @pl.when(j + s < 4)
-        def _(s=s):
-            dv_copy(s).wait_recv()
-            dv_acc[...] += dv_in[s].astype(jnp.float32)
+        dv_copy(s).wait_recv()
+        dv_acc[...] += dv_in[s].astype(jnp.float32)
 
     def gr_copy(s):
         return pltpu.make_async_remote_copy(
@@ -349,22 +326,22 @@
             dst_ref=gr_in.at[s],
             send_sem=gr_send.at[s],
             recv_sem=gr_recv.at[s],
-            device_id={"fsdp": (j + s) % 4 * 4 + g},
+            device_id=at((j + s) % 4, g),
             device_id_type=MESH,
         )
 
     dv_low = dv_acc[...].astype(jnp.bfloat16)
 
-    def rows_of(quarter):
-        first = pl.multiple_of(quarter * 4 * ROWS, 16)
-        return jnp.dot(
-            x_t[pl.ds(first, 4 * ROWS), :], dv_low, preferred_element_type=jnp.float32
-        )
-
-    for s in range(1, 4):
-        gr_out[s] = rows_of((j + s) % 4).astype(jnp.bfloat16)
+    def rows_of(quarter, i):
+        first = pl.multiple_of((i * QUARTERS + quarter) * ROWS, 16)
+        return jnp.dot(x_t[pl.ds(first, ROWS), :], dv_low, preferred_element_type=jnp.float32)
+
+    for s in range(1, 4):
+        for i in range(4):
+            gr_out[s, i * ROWS : (i + 1) * ROWS] = rows_of((j + s) % 4, i).astype(jnp.bfloat16)
         gr_copy(s).start()
-    gr_acc[...] = rows_of(j)
+    for i in range(4):
+        gr_acc[i * ROWS : (i + 1) * ROWS] = rows_of(j, i)
 
     pick(1)
     pick(2)
@@ -381,7 +358,7 @@
             dst_ref=grad.at[g],
             send_sem=own_send.at[s],
             recv_sem=own_recv.at[s],
-            device_id={"fsdp": j * 4 + peer},
+            device_id=at(j, peer),
             device_id_type=MESH,
         )
 
@@ -395,7 +372,7 @@
             dst_ref=slot,
             send_sem=own_send.at[s],
             recv_sem=own_recv.at[s],
-            device_id={"fsdp": j * 4 + (g + s) % 4},
+            device_id=at(j, (g + s) % 4),
             device_id_type=MESH,
         ).wait_recv()
 
@@ -415,22 +392,13 @@
     source_copy.start()
 
     for s in range(1, 4):
-        for kind in range(3):
+        for kind in range(4):
             group_copy(kind, s).wait_send()
 
-        @pl.when(j + s < 4)
-        def _(s=s):
-            key_copy(s).wait_send()
-
-        @pl.when(j >= s)
-        def _(s=s):
-            dv_copy(s).wait_send()
-
+        key_copy(s).wait_send()
+        dv_copy(s).wait_send()
         gr_copy(s).wait_send()
         own_copy(s).wait_send()
-    x_copy(g, sibling, 0).wait_send()
-    x_copy(g, (g + 2) % 4, 1).wait_send()
-    x_copy((g + 2) % 4, sibling, 2).wait_send()
 
     for part in range(3):
         sorts(
@@ -513,8 +481,6 @@
             dma((4,)),
             dma((4,)),
             dma((4,)),
-            dma((4,)),
-            dma((4,)),
             dma((3,)),
             dma((3,)),
             dma((3,)),

time: 89.4 us -> 85 us (0.951)
  Pallas kernels: 87.7 us -> 83.7 us
    pallas_call x1, Pallas kernels: 85.1 us -> 81.1 us  [local(): pl.pallas_call(kernel, out_shape=(jax.ShapeDtypeStruct((4, ROWS, HEAD_DIM...]
where the time goes in v3:
time: 85 us; the launch traced here: 84.3 us
  Pallas kernels  83.7 us (98%)
    pallas_call x1, Pallas kernels, local(): pl.pallas_call(kernel, out_shape=(jax.ShapeDtypeStruct((4, ROWS, HEAD_DIM...  81.1 us
    pallas_call x1, Pallas kernels, local(): pl.pallas_call(adam_kernel, out_shape=(jax.ShapeDtypeStruct((ROWS, KVW),...  2.56 us

profile of v3, /device:TPU:7, one launch (start us, length us, event | category | flops | bytes accessed | tf_op | source)
XLA Modules:
  0.0 84.3 jit_solution(5264466944096140791)
XLA Ops:
  0.6 81.1 %shard_map.103 = (bf16[4,112,256]{2,1,0:T(8,128)(2,1)}, bf16[8,336,128]{2,1,0:T(8,128)(2,1)}) custom-call(s32[32]{0:T(128)} %winners.1, bf16[128,1792]{1,0:T(8,128)(2,1)} %bitcast.12, bf16[128,2048]{1,0:T(8,128)(2,1)} %bitcast.10, bf16[128,1024]{1,0:T(8,128)(2,1)} %bitcast.17, bf16[128,2048]{1,0:T(8,128)(2,1)} %bitcast.11, bf16[112,1024]{1,0:T(8,128)(2,1)} %bitcast.18, ...), custom_call_target="tpu_custom_call" | custom-call | flops 3000000000 | bytes 6000000 | tf_op jit(solution)/shard_map/pallas_call | solution.py:435
  81.7 2.6 %shard_map.104 = (bf16[112,1024]{1,0:T(8,128)(2,1)}, f32[112,1024]{1,0:T(8,128)}, f32[112,1024]{1,0:T(8,128)}) custom-call(bf16[4,112,256]{2,1,0:T(8,128)(2,1)} %get-tuple-element.8.grad, bf16[8,336,128]{2,1,0:T(8,128)(2,1)} %get-tuple-element.9.source), custom_call_target="tpu_custom_call" | custom-call | tf_op jit(solution)/shard_map/pallas_call | solution.py:499

commit v4 on v3

v4 whole, which is shorter than its diff:
```python
import jax
import jax.numpy as jnp
from jax import lax
from jax.experimental import pallas as pl
from jax.experimental.pallas import tpu as pltpu
from jax.sharding import PartitionSpec as P

MEMBERS = 32
KV_HEADS = 4
QUARTERS = 4
HEAD_DIM = 256
GROUP_HEADS = 2
TOK = 128
FEAT = 1792
X_HALF = 896
ROWS = 112
KVW = 1024
PART = QUARTERS * TOK
PIECE = 80
RING = 16
HALF = 8
SLOTS = 5
BLOCKS = 7

beta_one = 0.9
beta_two = 0.999
learning_rate = 0.001
decay_rate = 0.1
adam_eps = 1e-08
adam_step = 200
soft_cap = 50.0

VMEM_LIMIT = 60 * 1024 * 1024

MESH = pl.DeviceIdType.MESH


def kernel(
    winners, x_in, q_in, k_in, c_in, w_in, m_in, v_in,
    grad_out, source_out, flag_out,
    k_all, q_g, c_g, x_g, x_t, expo, denom, cots,
    dv_acc, dv_out, dv_in, gr_acc, gr_out, gr_in, sum_out, grad,
    w_own, m_own, v_own, state, source, table_v, table_s,
    loc_sem, own_sem, out_sem, grp_send, grp_recv, key_send, key_recv, dv_send, dv_recv,
    gr_send, gr_recv, own_send, own_recv, x_send, x_recv, deal_send, deal_recv, swap_send, swap_recv,
    pick_send, pick_recv, *parts,
):
    me = lax.axis_index("member")
    mine = lax.axis_index("fsdp")
    dealt, swap_out, swap_in, sent = (
        [(parts[8 * part + 2 * kind], parts[8 * part + 2 * kind + 1]) for part in range(3)]
        for kind in range(4)
    )
    both = parts[24:27]
    g = mine // QUARTERS
    j = mine % QUARTERS

    def at(quarter, head):
        return {"fsdp": head * QUARTERS + quarter}

    state_copies = [
        pltpu.make_async_copy(src, dst, own_sem.at[i])
        for i, (src, dst) in enumerate(((w_in, w_own), (m_in, m_own), (v_in, v_own)))
    ]
    for copy in state_copies:
        copy.start()

    barrier = pltpu.get_barrier_semaphore()
    for s in range(1, 4):
        pl.semaphore_signal(
            barrier, inc=1, device_id=at(j, (g + s) % 4), device_id_type=MESH
        )
        pl.semaphore_signal(
            barrier, inc=1, device_id=at((j + s) % 4, g), device_id_type=MESH
        )

    def greet(offset, row):
        pl.semaphore_signal(
            barrier,
            inc=1,
            device_id={
                "member": (me // RING + row) % 2 * RING + (me + RING + offset) % RING
            },
            device_id_type=MESH,
        )

    @pl.loop(1, 6)
    def _(s):
        for row in range(2):
            greet(s, row)
            greet(-s, row)

    greet(0, 1)

    def own_slot(kind, owner):
        rows = pl.ds(owner * TOK, TOK)
        return (k_all.at[j, rows], q_g.at[rows], c_g.at[rows], x_g.at[rows])[kind]

    def own_slice(kind, head):
        if kind == 0:
            return k_in.at[:, pl.ds(head * HEAD_DIM, HEAD_DIM)]
        if kind == 3:
            return x_in
        wide = GROUP_HEADS * HEAD_DIM
        return (q_in, c_in)[kind - 1].at[:, pl.ds(head * wide, wide)]

    def group_copy(kind, s):
        peer = (g + s) % 4
        return pltpu.make_async_remote_copy(
            src_ref=own_slice(kind, peer),
            dst_ref=own_slot(kind, g),
            send_sem=grp_send.at[kind, s],
            recv_sem=grp_recv.at[kind, s],
            device_id=at(j, peer),
            device_id_type=MESH,
        )

    def group_wait(kind):
        for s in range(1, 4):
            slot = own_slot(kind, (g + 4 - s) % 4)
            pltpu.make_async_remote_copy(
                src_ref=slot,
                dst_ref=slot,
                send_sem=grp_send.at[kind, s],
                recv_sem=grp_recv.at[kind, s],
                device_id=at(j, (g + s) % 4),
                device_id_type=MESH,
            ).wait_recv()
        local_copy(kind).wait()

    def local_copy(kind):
        return pltpu.make_async_copy(own_slice(kind, g), own_slot(kind, g), loc_sem.at[kind])

    for kind in range(4):
        local_copy(kind).start()

    for copy in state_copies:
        copy.wait()
    for band in range(8):
        cols = slice(band * 128, (band + 1) * 128)
        state[band, 0:ROWS] = w_own[:, cols]
        state[band, ROWS : 2 * ROWS] = m_own[:, cols].astype(jnp.bfloat16)
        state[band, 2 * ROWS : 3 * ROWS] = v_own[:, cols].astype(jnp.bfloat16)

    pl.semaphore_wait(barrier, 6 + 21)

    for kind in range(3):
        for s in range(1, 4):
            group_copy(kind, s).start()

    core = mine % 2
    y = me // RING
    z = me % RING
    starts, sizes = (0, 48, 80), (48, 32, 16)
    cuts = ((z + RING - 5) % RING, (z + RING - 10) % RING)
    reach = (5, 2)

    def special(r):
        return (r + 2 * core) % 4 == 1

    def has(part, r, action):
        if part < 2:
            action()
        else:
            pl.when(special(r))(action)

    def place(ref, r, part, row=None):
        piece = (y if row is None else row) * RING + r
        first = piece % 4 * PIECE + starts[part] if part < 2 else 4 * PIECE
        return ref.at[piece // 4, pl.ds(first, sizes[part])]

    def bulk(part, count, send_sem, recv_sem):
        ref = sent[part][0].at[pl.ds(0, 15)] if count == 15 else both[part].at[pl.ds(0, count)]
        return pltpu.make_async_remote_copy(
            src_ref=ref,
            dst_ref=ref,
            send_sem=send_sem,
            recv_sem=recv_sem,
            device_id={"member": (me + 1) % MEMBERS},
            device_id_type=MESH,
        )

    def in_all(part, wait):
        if part < 2:
            wait(30)
        else:
            either = special(cuts[0]) | special(cuts[1])
            pl.when(either)(lambda: wait(7))
            pl.when(jnp.logical_not(either))(lambda: wait(8))

    def deal(part):
        @pl.loop(0, HALF)
        def _(d):
            for role in range(2):
                r = (z + RING - HALF * role - d) % RING
                for row in range(2):

                    def start(role=role, row=row, r=r):
                        pltpu.make_async_remote_copy(
                            src_ref=place(state, r, part, row),
                            dst_ref=dealt[part][role].at[y * HALF + d],
                            send_sem=deal_send.at[part],
                            recv_sem=deal_recv.at[part, role],
                            device_id={
                                "member": row * RING + (z + RING + reach[role] - d) % RING
                            },
                            device_id_type=MESH,
                        ).start()

                    other = (d != reach[role]) | (y != row)
                    pl.when(other if part < 2 else other & special(r))(start)

        for role in range(2):

            def keep(role=role):
                dealt[part][role][y * HALF + reach[role]] = place(state, cuts[role], part)[...]

            has(part, cuts[role], keep)

    def slot(member, role):
        return member // RING * HALF + (member % RING + RING - cuts[role]) % HALF

    def swap_copy(part, role):
        partner = (z + 5) % RING if role == 0 else (z + RING - 5) % RING
        return pltpu.make_async_remote_copy(
            src_ref=swap_out[part][role],
            dst_ref=swap_in[part][1 - role],
            send_sem=swap_send.at[part, role],
            recv_sem=swap_recv.at[part, 1 - role],
            device_id={"member": y * RING + partner},
            device_id_type=MESH,
        )

    def swap(part):
        for role in range(2):

            def action(role=role):
                bulk(part, 15, deal_send.at[part], deal_recv.at[part, role]).wait_recv()
                for k in range(SLOTS):
                    swap_out[part][role][k] = dealt[part][role][slot(table_s[2 * role, k], role)]
                swap_copy(part, role).start()

            has(part, cuts[role], action)

    def serve(part):
        for role in range(2):

            def action(role=role):
                swap_copy(part, 1 - role).wait_recv()

                @pl.loop(0, HALF)
                def _(d):
                    for row in range(2):
                        member = row * RING + (z + RING - reach[role] + d) % RING
                        winner = winners[member]
                        inside = (winner % RING + RING - cuts[role]) % RING // HALF == role
                        near = dealt[part][role][slot(winner, role)]
                        rank = jnp.minimum(table_s[2 * role + 1, winner], SLOTS - 1)
                        far = swap_in[part][role][rank]
                        sent[part][role][row * HALF + d] = jnp.where(inside, near, far)

                        def start(row=row, member=member):
                            pltpu.make_async_remote_copy(
                                src_ref=sent[part][role].at[row * HALF + d],
                                dst_ref=place(source, cuts[role], part),
                                send_sem=pick_send.at[part],
                                recv_sem=pick_recv.at[part],
                                device_id={"member": member},
                                device_id_type=MESH,
                            ).start()

                        pl.when((d != reach[role]) | (y != row))(start)

                place(source, cuts[role], part)[...] = sent[part][role][y * HALF + reach[role]]

            has(part, cuts[role], action)

    for part in range(3):
        deal(part)

    right, left = (g + 1) % 4, (g + 3) % 4
    routes = ((0, g, right), (0, g, left), (1, g, left), (1, g, right), (0, left, right), (1, right, left))
    x_from = (left, right, right, left, left, right)
    x_owner = (left, right, right, left, (g + 2) % 4, (g + 2) % 4)

    def x_slot(owner, half):
        return x_g.at[pl.ds(owner * TOK, TOK), pl.ds(half * X_HALF, X_HALF)]

    def x_copy(route):
        half, owner, peer = routes[route]
        slot = x_slot(owner, half)
        return pltpu.make_async_remote_copy(
            src_ref=slot if route > 3 else x_in.at[:, pl.ds(half * X_HALF, X_HALF)],
            dst_ref=slot,
            send_sem=x_send.at[route],
            recv_sem=x_recv.at[route],
            device_id=at(j, peer),
            device_id_type=MESH,
        )

    def x_wait(route):
        slot = x_slot(x_owner[route], routes[route][0])
        pltpu.make_async_remote_copy(
            src_ref=slot,
            dst_ref=slot,
            send_sem=x_send.at[route],
            recv_sem=x_recv.at[route],
            device_id=at(j, x_from[route]),
            device_id_type=MESH,
        ).wait_recv()

    for route in range(4):
        x_copy(route).start()

    shape = (MEMBERS, 128)
    sub = lax.broadcasted_iota(jnp.int32, shape, 0)
    lane = lax.broadcasted_iota(jnp.int32, shape, 1)
    by_sub = jnp.zeros(shape, jnp.int32)
    by_lane = jnp.full(shape, -1, jnp.int32)
    for b in range(MEMBERS):
        by_sub = jnp.where(sub == b, winners[b], by_sub)
        by_lane = jnp.where(lane == b, winners[b], by_lane)
    one, none = jnp.ones(shape, jnp.int32), jnp.zeros(shape, jnp.int32)
    takes = jnp.where(by_lane == sub, one, none)
    taken = jnp.where(by_sub == lane, one, none)

    def inside_of(index, r, role):
        return jnp.where((index % RING + RING - r) % RING // HALF == role, one, none)

    def needed_by(r, role):
        in_sub, in_lane = inside_of(sub, r, role), inside_of(lane, r, role)
        out_sub = in_sub * jnp.max(takes * (1 - in_lane), axis=1, keepdims=True)
        return in_sub, in_lane, out_sub

    for role in range(2):
        in_sub, in_lane, out_sub = needed_by(cuts[role], role)
        out_lane = in_lane * jnp.max(taken * (1 - in_sub), axis=0, keepdims=True)
        rank = jnp.sum(jnp.where(lane < sub, out_lane, none), axis=1, keepdims=True)
        chosen = jnp.where(rank == lane, out_sub * sub, none)
        table_v[2 * role : 2 * role + 1, :] = jnp.sum(chosen, axis=0, keepdims=True)
        in_need = (1 - in_sub) * jnp.max(takes * in_lane, axis=1, keepdims=True)
        table_v[2 * role + 1 : 2 * role + 2, :] = jnp.sum(
            jnp.where(sub < lane, in_need, none), axis=0, keepdims=True
        )
    table_copy = pltpu.make_async_copy(table_v, table_s, out_sem.at[2])
    table_copy.start()

    most = jnp.zeros((1, 128), jnp.int32)
    for r in range(RING):
        most = jnp.maximum(most, jnp.sum(needed_by(r, 0)[2], axis=0, keepdims=True))
    flag_out[0] = jnp.max(jnp.where(most > SLOTS, 1, 0))
    table_copy.wait()

    def key_copy(s):
        return pltpu.make_async_remote_copy(
            src_ref=k_all.at[j],
            dst_ref=k_all.at[j],
            send_sem=key_send.at[s],
            recv_sem=key_recv.at[s],
            device_id=at((j + s) % 4, g),
            device_id_type=MESH,
        )

    def key_wait(s):
        slot = k_all.at[(j + 4 - s) % 4]
        pltpu.make_async_remote_copy(
            src_ref=slot,
            dst_ref=slot,
            send_sem=key_send.at[s],
            recv_sem=key_recv.at[s],
            device_id=at((j + s) % 4, g),
            device_id_type=MESH,
        ).wait_recv()

    group_wait(0)
    for s in range(1, 4):
        key_copy(s).start()

    group_wait(1)
    denom[...] = jnp.zeros_like(denom)

    def scores(chunk):
        later = jnp.where(chunk > j, TOK, jnp.where(chunk < j, -TOK, 0))
        for i in range(4):
            first = i * TOK
            key_block = k_all[chunk, first : first + TOK, :]
            for h in range(GROUP_HEADS):
                raw = lax.dot_general(
                    key_block,
                    q_g[first:PART, h * HEAD_DIM : (h + 1) * HEAD_DIM],
                    (((1,), (1,)), ((), ())),
                    preferred_element_type=jnp.float32,
                )
                e = jnp.exp(soft_cap * jnp.tanh(raw * (HEAD_DIM**-0.5 / soft_cap)))
                u = lax.broadcasted_iota(jnp.int32, raw.shape, 0)
                t = lax.broadcasted_iota(jnp.int32, raw.shape, 1)
                e = jnp.where((u + later <= t) | (t >= TOK), e, 0.0)
                cols = slice(h * PART + first, (h + 1) * PART)
                expo[chunk, first : first + TOK, cols] = e.astype(jnp.bfloat16)
                denom[:, cols] += jnp.sum(e, axis=0, keepdims=True)

    scores(j)
    swap(0)

    @pl.loop(1, 4)
    def _(s):
        key_wait(s)
        scores((j + 4 - s) % 4)

    swap(1)
    swap(2)

    group_wait(2)
    for h in range(GROUP_HEADS):
        cols = slice(h * PART, (h + 1) * PART)
        inverse = jnp.transpose(jnp.broadcast_to(1.0 / denom[:, cols], (128, PART)))
        heads = c_g[:, h * HEAD_DIM : (h + 1) * HEAD_DIM].astype(jnp.float32)
        for half in range(2):
            lanes = slice(half * 128, (half + 1) * 128)
            cots[cols, lanes] = (heads[:, lanes] * inverse).astype(jnp.bfloat16)

    def dv_copy(s):
        return pltpu.make_async_remote_copy(
            src_ref=dv_out.at[s],
            dst_ref=dv_in.at[s],
            send_sem=dv_send.at[s],
            recv_sem=dv_recv.at[s],
            device_id=at((j + 4 - s) % 4, g),
            device_id_type=MESH,
        )

    def dv_rows(chunk, i):
        first = i * TOK
        total = None
        for h in range(GROUP_HEADS):
            cols = slice(h * PART + first, (h + 1) * PART)
            term = jnp.dot(
                expo[chunk, first : first + TOK, cols],
                cots[cols, :],
                preferred_element_type=jnp.float32,
            )
            total = term if total is None else total + term
        return total

    @pl.loop(1, 4)
    def _(s):
        for i in range(4):
            dv_out[s, i * TOK : (i + 1) * TOK] = dv_rows((j + 4 - s) % 4, i).astype(jnp.bfloat16)
        dv_copy(s).start()

    for i in range(4):
        dv_acc[i * TOK : (i + 1) * TOK] = dv_rows(j, i)

    x_wait(0)
    x_copy(4).start()
    x_wait(2)
    x_copy(5).start()

    serve(0)

    local_copy(3).wait()

    def turn(half):
        for route in ((1, 4), (3, 5))[half]:
            x_wait(route)

        @pl.loop(0, X_HALF // 128)
        def _(i):
            first = pl.multiple_of(half * X_HALF + i * 128, 128)
            x_t[pl.ds(first, 128), :] = jnp.transpose(x_g[:, pl.ds(first, 128)])

    turn(0)

    for s in range(1, 4):
        dv_copy(s).wait_recv()
        dv_acc[...] += dv_in[s].astype(jnp.float32)

    def gr_copy(s, half):
        rows = pl.ds(half * 2 * ROWS, 2 * ROWS)
        return pltpu.make_async_remote_copy(
            src_ref=gr_out.at[s, rows],
            dst_ref=gr_in.at[s, rows],
            send_sem=gr_send.at[half, s],
            recv_sem=gr_recv.at[half, s],
            device_id=at((j + s) % 4, g),
            device_id_type=MESH,
        )

    dv_low = dv_acc[...].astype(jnp.bfloat16)

    def rows_of(quarter, i):
        first = pl.multiple_of((i * QUARTERS + quarter) * ROWS, 16)
        return jnp.dot(x_t[pl.ds(first, ROWS), :], dv_low, preferred_element_type=jnp.float32)

    def spread(half):
        blocks = (2 * half, 2 * half + 1)
        for s in range(1, 4):
            for i in blocks:
                gr_out[s, i * ROWS : (i + 1) * ROWS] = rows_of((j + s) % 4, i).astype(jnp.bfloat16)
            gr_copy(s, half).start()
        for i in blocks:
            gr_acc[i * ROWS : (i + 1) * ROWS] = rows_of(j, i)

    def own_copy(i):
        return pltpu.make_async_remote_copy(
            src_ref=sum_out.at[pl.ds(i * ROWS, ROWS)],
            dst_ref=grad.at[g],
            send_sem=own_send.at[i],
            recv_sem=own_recv.at[g],
            device_id=at(j, i),
            device_id_type=MESH,
        )

    def deliver(half):
        rows = slice(half * 2 * ROWS, (half + 1) * 2 * ROWS)
        total = gr_acc[rows]
        for s in range(1, 4):
            gr_copy(s, half).wait_recv()
            total += gr_in[s, rows].astype(jnp.float32)
        sum_out[rows] = total.astype(jnp.bfloat16)
        for i in (2 * half, 2 * half + 1):
            pl.when(g != i)(lambda: own_copy(i).start())

            @pl.when(g == i)
            def _(i=i):
                grad[i] = sum_out[i * ROWS : (i + 1) * ROWS]

    spread(0)
    serve(1)
    serve(2)
    turn(1)
    spread(1)
    deliver(0)
    deliver(1)

    for s in range(1, 4):
        peer = (g + s) % 4
        slot = grad.at[peer]
        pltpu.make_async_remote_copy(
            src_ref=slot,
            dst_ref=slot,
            send_sem=own_send.at[peer],
            recv_sem=own_recv.at[peer],
            device_id=at(j, peer),
            device_id_type=MESH,
        ).wait_recv()

    grad_copy = pltpu.make_async_copy(grad, grad_out, out_sem.at[0])
    grad_copy.start()

    for part in range(3):
        in_all(
            part,
            lambda n: bulk(part, n, deal_send.at[part], pick_recv.at[part]).wait_send(),
        )
        for role in range(2):
            has(part, cuts[role], lambda: swap_copy(part, role).wait_send())
    for part in range(3):
        in_all(
            part,
            lambda n: bulk(part, n, deal_send.at[part], pick_recv.at[part]).wait_recv(),
        )

    source_copy = pltpu.make_async_copy(source, source_out, out_sem.at[1])
    source_copy.start()

    for s in range(1, 4):
        for kind in range(3):
            group_copy(kind, s).wait_send()

        key_copy(s).wait_send()
        dv_copy(s).wait_send()
        gr_copy(s, 0).wait_send()
        gr_copy(s, 1).wait_send()
        own_copy((g + s) % 4).wait_send()
    for route in range(6):
        x_copy(route).wait_send()

    for part in range(3):
        for role in range(2):
            has(
                part,
                cuts[role],
                lambda: bulk(part, 15, pick_send.at[part], pick_recv.at[part]).wait_send(),
            )

    grad_copy.wait()
    source_copy.wait()


def plain_exchange(
    winners, w_in, m_in, v_in, source_out,
    w_own, m_own, v_own, state, dealt_0, dealt_1, dealt_2, picked_0, picked_1, picked_2, source,
    own_sem, out_sem, deal_send, deal_recv, pick_send, pick_recv,
):
    me = lax.axis_index("member")
    mine = lax.axis_index("fsdp")

    state_copies = [
        pltpu.make_async_copy(src, dst, own_sem.at[i])
        for i, (src, dst) in enumerate(((w_in, w_own), (m_in, m_own), (v_in, v_own)))
    ]
    for copy in state_copies:
        copy.start()

    barrier = pltpu.get_barrier_semaphore()

    @pl.loop(1, MEMBERS)
    def _(s):
        pl.semaphore_signal(
            barrier, inc=1, device_id={"member": (me + s) % MEMBERS}, device_id_type=MESH
        )

    for copy in state_copies:
        copy.wait()
    for band in range(8):
        cols = slice(band * 128, (band + 1) * 128)
        state[band, 0:ROWS] = w_own[:, cols]
        state[band, ROWS : 2 * ROWS] = m_own[:, cols].astype(jnp.bfloat16)
        state[band, 2 * ROWS : 3 * ROWS] = v_own[:, cols].astype(jnp.bfloat16)
    pl.semaphore_wait(barrier, MEMBERS - 1)

    core = mine % 2
    starts, sizes = (0, 48, 80), (48, 32, 16)
    dealt, picked = (dealt_0, dealt_1, dealt_2), (picked_0, picked_1, picked_2)

    def extra(member):
        return (member + 2 * core) % 4 == 1

    def sorts(member, part, action):
        if part < 2:
            action()
        else:
            pl.when(extra(member))(action)

    def place(ref, member, part):
        first = member % 4 * PIECE + starts[part] if part < 2 else 4 * PIECE
        return ref.at[member // 4, pl.ds(first, sizes[part])]

    def deal_copy(s, part):
        peer = (me + s) % MEMBERS
        return pltpu.make_async_remote_copy(
            src_ref=place(state, peer, part),
            dst_ref=dealt[part].at[me],
            send_sem=deal_send.at[part],
            recv_sem=deal_recv.at[part],
            device_id={"member": peer},
            device_id_type=MESH,
        )

    def all_of(part, count, send_sem, recv_sem):
        ref = dealt[part].at[pl.ds(0, count)]
        return pltpu.make_async_remote_copy(
            src_ref=ref,
            dst_ref=ref,
            send_sem=send_sem.at[part],
            recv_sem=recv_sem.at[part],
            device_id={"member": (me + 1) % MEMBERS},
            device_id_type=MESH,
        )

    def to_or_from_sorters(part, wait):
        if part < 2:
            wait(MEMBERS - 1)
        else:
            pl.when(extra(me))(lambda: wait(MEMBERS // 4 - 1))
            pl.when(jnp.logical_not(extra(me)))(lambda: wait(MEMBERS // 4))

    for part in range(3):

        @pl.loop(1, MEMBERS)
        def _(s):
            sorts((me + s) % MEMBERS, part, lambda: deal_copy(s, part).start())

    def keep(part):
        dealt[part][me] = place(state, me, part)[...]

    for part in range(3):
        sorts(me, part, lambda: keep(part))

    def pick_copy(s, part):
        peer = (me + s) % MEMBERS
        return pltpu.make_async_remote_copy(
            src_ref=picked[part].at[s],
            dst_ref=place(source, me, part),
            send_sem=pick_send.at[part],
            recv_sem=pick_recv.at[part],
            device_id={"member": peer},
            device_id_type=MESH,
        )

    def pick(part):
        def action():
            all_of(part, MEMBERS - 1, deal_send, deal_recv).wait_recv()

            @pl.loop(1, MEMBERS)
            def _(s):
                picked[part][s] = dealt[part][winners[(me + s) % MEMBERS]]
                pick_copy(s, part).start()

            place(source, me, part)[...] = dealt[part][winners[me]]

        sorts(me, part, action)

    for part in range(3):
        pick(part)
    for part in range(3):
        to_or_from_sorters(
            part, lambda count: all_of(part, count, deal_send, deal_recv).wait_send()
        )
    for part in range(3):
        to_or_from_sorters(
            part, lambda count: all_of(part, count, pick_send, pick_recv).wait_recv()
        )

    source_copy = pltpu.make_async_copy(source, source_out, out_sem.at[0])
    source_copy.start()
    for part in range(3):
        sorts(
            me, part, lambda: all_of(part, MEMBERS - 1, pick_send, pick_recv).wait_send()
        )
    source_copy.wait()


def adam_kernel(grad, source, new_w, new_m, new_v):
    for band in range(8):
        cols = slice(band * 128, (band + 1) * 128)
        lanes = slice(band % 2 * 128, band % 2 * 128 + 128)
        gradient = grad[band // 2, :, lanes].astype(jnp.float32)
        old_w = source[band, 0:ROWS].astype(jnp.float32)
        old_m = source[band, ROWS : 2 * ROWS].astype(jnp.float32)
        old_v = source[band, 2 * ROWS : 3 * ROWS].astype(jnp.float32)
        first = beta_one * old_m + (1.0 - beta_one) * gradient
        second = beta_two * old_v + (1.0 - beta_two) * gradient * gradient
        first_hat = first * (1.0 / (1.0 - beta_one**adam_step))
        second_hat = second * (1.0 / (1.0 - beta_two**adam_step))
        update = first_hat / (jnp.sqrt(second_hat) + adam_eps) + decay_rate * old_w
        new_w[:, cols] = (old_w - learning_rate * update).astype(jnp.bfloat16)
        new_m[:, cols] = first
        new_v[:, cols] = second


def local(inputs, queries, keys, cotangent, winners, weights, first_moment, second_moment):
    f32, bf16 = jnp.float32, jnp.bfloat16
    vmem = pl.BlockSpec(memory_space=pltpu.VMEM)
    hbm = pl.BlockSpec(memory_space=pltpu.HBM)
    dma = pltpu.SemaphoreType.DMA
    scratch = [
        pltpu.VMEM((QUARTERS, PART, HEAD_DIM), bf16),
        pltpu.VMEM((PART, GROUP_HEADS * HEAD_DIM), bf16),
        pltpu.VMEM((PART, GROUP_HEADS * HEAD_DIM), bf16),
        pltpu.VMEM((PART, FEAT), bf16),
        pltpu.VMEM((FEAT, PART), bf16),
        pltpu.VMEM((QUARTERS, PART, GROUP_HEADS * PART), bf16),
        pltpu.VMEM((1, GROUP_HEADS * PART), f32),
        pltpu.VMEM((GROUP_HEADS * PART, HEAD_DIM), bf16),
        pltpu.VMEM((PART, HEAD_DIM), f32),
        pltpu.VMEM((4, PART, HEAD_DIM), bf16),
        pltpu.VMEM((4, PART, HEAD_DIM), bf16),
        pltpu.VMEM((4 * ROWS, HEAD_DIM), f32),
        pltpu.VMEM((4, 4 * ROWS, HEAD_DIM), bf16),
        pltpu.VMEM((4, 4 * ROWS, HEAD_DIM), bf16),
        pltpu.VMEM((4 * ROWS, HEAD_DIM), bf16),
        pltpu.VMEM((4, ROWS, HEAD_DIM), bf16),
    ]
    own_state = [
        pltpu.VMEM((ROWS, KVW), bf16),
        pltpu.VMEM((ROWS, KVW), f32),
        pltpu.VMEM((ROWS, KVW), f32),
        pltpu.VMEM((8, 3 * ROWS, 128), bf16),
    ]
    landing = pltpu.VMEM((8, 3 * ROWS, 128), bf16)
    parts = []
    for rows in (48, 32, 16):
        for count in (16, SLOTS, SLOTS, 16):
            parts += [pltpu.VMEM((count, rows, 128), bf16)] * 2
    parts += [pltpu.VMEM((30, rows, 128), bf16) for rows in (48, 32, 16)]
    state_args = (weights[0], first_moment[0], second_moment[0])
    state_shape = jax.ShapeDtypeStruct((8, 3 * ROWS, 128), bf16)
    smem = pl.BlockSpec(memory_space=pltpu.SMEM)
    grad, source, flag = pl.pallas_call(
        kernel,
        out_shape=(
            jax.ShapeDtypeStruct((4, ROWS, HEAD_DIM), bf16),
            state_shape,
            jax.ShapeDtypeStruct((1,), jnp.int32),
        ),
        in_specs=[smem] + [hbm] * 7,
        out_specs=(hbm, hbm, smem),
        scratch_shapes=scratch
        + own_state
        + [landing, pltpu.VMEM((8, 128), jnp.int32), pltpu.SMEM((8, 128), jnp.int32)]
        + [dma((4,)), dma((3,)), dma((3,)), dma((4, 4)), dma((4, 4))]
        + [dma((4,))] * 4
        + [dma((2, 4)), dma((2, 4)), dma((4,)), dma((4,)), dma((6,)), dma((6,))]
        + [dma((3,)), dma((3, 2)), dma((3, 2)), dma((3, 2)), dma((3,)), dma((3,))]
        + parts,
        compiler_params=pltpu.CompilerParams(
            collective_id=0, has_side_effects=True, vmem_limit_bytes=VMEM_LIMIT
        ),
        cost_estimate=pl.CostEstimate(
            flops=3_000_000_000, bytes_accessed=6_000_000, transcendentals=4_000_000
        ),
    )(winners, inputs[0], queries[0], keys[0], cotangent[0], *state_args)

    def step(grad, source):
        return pl.pallas_call(
            adam_kernel,
            out_shape=(
                jax.ShapeDtypeStruct((ROWS, KVW), bf16),
                jax.ShapeDtypeStruct((ROWS, KVW), f32),
                jax.ShapeDtypeStruct((ROWS, KVW), f32),
            ),
            in_specs=[vmem, vmem],
            out_specs=(vmem, vmem, vmem),
            compiler_params=pltpu.CompilerParams(vmem_limit_bytes=VMEM_LIMIT),
        )(grad, source)

    def crowded():
        all_source = pl.pallas_call(
            plain_exchange,
            out_shape=state_shape,
            in_specs=[smem] + [hbm] * 3,
            out_specs=hbm,
            scratch_shapes=own_state
            + [pltpu.VMEM((MEMBERS, rows, 128), bf16) for rows in (48, 32, 16)] * 2
            + [landing, dma((3,)), dma((1,))]
            + [dma((3,))] * 4,
            compiler_params=pltpu.CompilerParams(
                collective_id=1, has_side_effects=True, vmem_limit_bytes=VMEM_LIMIT
            ),
        )(winners, *state_args)
        return step(grad, all_source)

    outs = lax.cond(flag[0] > 0, crowded, lambda: step(grad, source))
    return tuple(out[None] for out in outs)


def solution(mesh):
    rows = P("member", "fsdp", None)
    return jax.shard_map(
        local,
        mesh=mesh,
        in_specs=(rows, rows, rows, rows, P(), rows, rows, rows),
        out_specs=(rows, rows, rows),
        check_vma=False,
    )
```

time: 85 us -> 79.7 us (0.938)
  Pallas kernels: 83.7 us -> 77.5 us
    pallas_call x1, Pallas kernels: 81.1 us -> 76.2 us  [local(): pl.pallas_call(kernel, out_shape=(jax.ShapeDtypeStruct((4, ROWS, HEAD_DIM...]
    pallas_call x1, Pallas kernels: 2.56 us -> 1.33 us  [step(): pl.pallas_call(adam_kernel, out_shape=(jax.ShapeDtypeStruct((ROWS, KVW),...]
where the time goes in v4:
time: 79.7 us; the launch traced here: 79.5 us
  Pallas kernels  77.5 us (97%)
  between operations  1.36 us (2%)
    pallas_call x1, Pallas kernels, local(): pl.pallas_call(kernel, out_shape=(jax.ShapeDtypeStruct((4, ROWS, HEAD_DIM...  76.2 us

profile of v4, /device:TPU:7, one launch (start us, length us, event | category | flops | bytes accessed | tf_op | source)
XLA Modules:
  0.0 79.5 jit_solution(11632342520791054300)
XLA Ops:
  0.6 0.0 copy-start.3
  0.6 0.6 copy-done.3
  1.3 0.0 copy-start
  1.3 0.0 copy-start.1
  1.3 0.0 copy-start.2
  1.3 76.2 %shard_map.103 = (bf16[4,112,256]{2,1,0:T(8,128)(2,1)S(1)}, bf16[8,336,128]{2,1,0:T(8,128)(2,1)S(1)}, s32[1]{0:T(128)}) custom-call(s32[32]{0:T(128)S(1)} %copy-done.3, bf16[128,1792]{1,0:T(8,128)(2,1)} %bitcast.19, bf16[128,2048]{1,0:T(8,128)(2,1)} %bitcast.17, bf16[128,1024]{1,0:T(8,128)(2,1)} %bitcast.22, bf16[128,2048]{1,0:T(8,128)(2,1)} %bitcast.18, ...), custom_call_target="tpu_custom_call" | custom-call | flops 3000000000 | bytes 6000000 | tf_op jit(solution)/shard_map/pallas_call | solution.py:781
  78.2 0.0 copy-done
  78.2 0.0 copy-done.1
  78.2 0.0 copy-done.2
  78.2 1.3 %conditional.1 = ((bf16[112,1024]{1,0:T(8,128)(2,1)}, f32[112,1024]{1,0:T(8,128)}, f32[112,1024]{1,0:T(8,128)})) conditional(s32[]{:T(128)} %bitcast.7, (bf16[4,112,256]{2,1,0:T(8,128)(2,1)S(1)}, bf16[8,336,128]{2,1,0:T(8,128)(2,1)S(1)}) %tuple.21, (s32[32]{0:T(128)S(1)}, bf16[112,1024]{1,0:T(8,128)(2,1)S(1)}, f32[112,1024]{1,0:T(8,128)S(1)}, ...), branch_computations={%region_0.0_spmd.clone, %region_1.0_spmd.clone} | conditional | bytes 8 | solution.py:835
  78.2 1.3 %branch_0_fun.1 = (bf16[112,1024]{1,0:T(8,128)(2,1)}, f32[112,1024]{1,0:T(8,128)}, f32[112,1024]{1,0:T(8,128)}) custom-call(bf16[4,112,256]{2,1,0:T(8,128)(2,1)S(1)} %get-tuple-element.50.grad, bf16[8,336,128]{2,1,0:T(8,128)(2,1)S(1)} %get-tuple-element.51.source), custom_call_target="tpu_custom_call" | custom-call | tf_op jit(solution)/shard_map/cond/branch_0_fun/pallas_call | solution.py:807
Async XLA Ops:
  0.6 0.7 copy-start.3
  1.3 76.9 %copy-start = (f32[1,112,1024]{2,1,0:T(8,128)S(1)}, f32[1,112,1024]{2,1,0:T(8,128)}, u32[]{:S(2)}) copy-start(f32[1,112,1024]{2,1,0:T(8,128)} %param.16) | copy-start | bytes 1376260
  1.3 76.9 %copy-start.1 = (f32[1,112,1024]{2,1,0:T(8,128)S(1)}, f32[1,112,1024]{2,1,0:T(8,128)}, u32[]{:S(2)}) copy-start(f32[1,112,1024]{2,1,0:T(8,128)} %param.17) | copy-start | bytes 1376260
  1.3 76.9 %copy-start.2 = (bf16[1,112,1024]{2,1,0:T(8,128)(2,1)S(1)}, bf16[1,112,1024]{2,1,0:T(8,128)(2,1)}, u32[]{:S(2)}) copy-start(bf16[1,112,1024]{2,1,0:T(8,128)(2,1)} %param.15) | copy-start | bytes 688132

commit v5 on v4

--- a/solution.py
+++ b/solution.py
@@ -55,6 +55,10 @@
     g = mine // QUARTERS
     j = mine % QUARTERS
 
+    sibling = j + 1 - 2 * (j % 2)
+    across = (j + 2) % QUARTERS
+    diagonal = (sibling + 2) % QUARTERS
+
     def at(quarter, head):
         return {"fsdp": head * QUARTERS + quarter}
 
@@ -134,6 +138,12 @@
     for kind in range(4):
         local_copy(kind).start()
 
+    pl.semaphore_wait(barrier, 6 + 21)
+
+    for kind in range(3):
+        for s in range(1, 4):
+            group_copy(kind, s).start()
+
     for copy in state_copies:
         copy.wait()
     for band in range(8):
@@ -141,12 +151,6 @@
         state[band, 0:ROWS] = w_own[:, cols]
         state[band, ROWS : 2 * ROWS] = m_own[:, cols].astype(jnp.bfloat16)
         state[band, 2 * ROWS : 3 * ROWS] = v_own[:, cols].astype(jnp.bfloat16)
-
-    pl.semaphore_wait(barrier, 6 + 21)
-
-    for kind in range(3):
-        for s in range(1, 4):
-            group_copy(kind, s).start()
 
     core = mine % 2
     y = me // RING
@@ -217,7 +221,7 @@
 
             has(part, cuts[role], keep)
 
-    def slot(member, role):
+    def seat(member, role):
         return member // RING * HALF + (member % RING + RING - cuts[role]) % HALF
 
     def swap_copy(part, role):
@@ -237,7 +241,7 @@
             def action(role=role):
                 bulk(part, 15, deal_send.at[part], deal_recv.at[part, role]).wait_recv()
                 for k in range(SLOTS):
-                    swap_out[part][role][k] = dealt[part][role][slot(table_s[2 * role, k], role)]
+                    swap_out[part][role][k] = dealt[part][role][seat(table_s[2 * role, k], role)]
                 swap_copy(part, role).start()
 
             has(part, cuts[role], action)
@@ -254,7 +258,7 @@
                         member = row * RING + (z + RING - reach[role] + d) % RING
                         winner = winners[member]
                         inside = (winner % RING + RING - cuts[role]) % RING // HALF == role
-                        near = dealt[part][role][slot(winner, role)]
+                        near = dealt[part][role][seat(winner, role)]
                         rank = jnp.minimum(table_s[2 * role + 1, winner], SLOTS - 1)
                         far = swap_in[part][role][rank]
                         sent[part][role][row * HALF + d] = jnp.where(inside, near, far)
@@ -351,30 +355,31 @@
     flag_out[0] = jnp.max(jnp.where(most > SLOTS, 1, 0))
     table_copy.wait()
 
-    def key_copy(s):
-        return pltpu.make_async_remote_copy(
-            src_ref=k_all.at[j],
-            dst_ref=k_all.at[j],
-            send_sem=key_send.at[s],
-            recv_sem=key_recv.at[s],
-            device_id=at((j + s) % 4, g),
-            device_id_type=MESH,
-        )
-
-    def key_wait(s):
-        slot = k_all.at[(j + 4 - s) % 4]
+    def key_copy(route):
+        slot = k_all.at[across if route == 2 else j]
+        return pltpu.make_async_remote_copy(
+            src_ref=slot,
+            dst_ref=slot,
+            send_sem=key_send.at[route],
+            recv_sem=key_recv.at[route],
+            device_id=at(across if route == 1 else sibling, g),
+            device_id_type=MESH,
+        )
+
+    def key_wait(route):
+        slot = k_all.at[(sibling, across, diagonal)[route]]
         pltpu.make_async_remote_copy(
             src_ref=slot,
             dst_ref=slot,
-            send_sem=key_send.at[s],
-            recv_sem=key_recv.at[s],
-            device_id=at((j + s) % 4, g),
+            send_sem=key_send.at[route],
+            recv_sem=key_recv.at[route],
+            device_id=at(across if route == 1 else sibling, g),
             device_id_type=MESH,
         ).wait_recv()
 
     group_wait(0)
-    for s in range(1, 4):
-        key_copy(s).start()
+    key_copy(1).start()
+    key_copy(0).start()
 
     group_wait(1)
     denom[...] = jnp.zeros_like(denom)
@@ -402,10 +407,14 @@
     scores(j)
     swap(0)
 
-    @pl.loop(1, 4)
+    key_wait(1)
+    key_copy(2).start()
+    key_wait(0)
+
+    @pl.loop(0, 3)
     def _(s):
-        key_wait(s)
-        scores((j + 4 - s) % 4)
+        pl.when(s == 2)(lambda: key_wait(2))
+        scores(jnp.where(s == 0, sibling, jnp.where(s == 1, across, diagonal)))
 
     swap(1)
     swap(2)
@@ -419,13 +428,13 @@
             lanes = slice(half * 128, (half + 1) * 128)
             cots[cols, lanes] = (heads[:, lanes] * inverse).astype(jnp.bfloat16)
 
-    def dv_copy(s):
-        return pltpu.make_async_remote_copy(
-            src_ref=dv_out.at[s],
-            dst_ref=dv_in.at[s],
-            send_sem=dv_send.at[s],
-            recv_sem=dv_recv.at[s],
-            device_id=at((j + 4 - s) % 4, g),
+    def dv_copy(slot):
+        return pltpu.make_async_remote_copy(
+            src_ref=dv_out.at[slot],
+            dst_ref=dv_in.at[slot],
+            send_sem=dv_send.at[slot],
+            recv_sem=dv_recv.at[slot],
+            device_id=at(across if slot == 2 else sibling, g),
             device_id_type=MESH,
         )
 
@@ -442,21 +451,30 @@
             total = term if total is None else total + term
         return total
 
-    @pl.loop(1, 4)
-    def _(s):
+    for slot, chunk in ((1, diagonal), (0, sibling)):
         for i in range(4):
-            dv_out[s, i * TOK : (i + 1) * TOK] = dv_rows((j + 4 - s) % 4, i).astype(jnp.bfloat16)
-        dv_copy(s).start()
-
-    for i in range(4):
-        dv_acc[i * TOK : (i + 1) * TOK] = dv_rows(j, i)
+            dv_out[slot, i * TOK : (i + 1) * TOK] = dv_rows(chunk, i).astype(jnp.bfloat16)
+        dv_copy(slot).start()
+
+    @pl.loop(0, 2)
+    def _(step):
+        chunk = jnp.where(step == 0, across, j)
+        for i in range(4):
+            dv_acc[step, i * TOK : (i + 1) * TOK] = dv_rows(chunk, i)
+
+    dv_copy(1).wait_recv()
+    dv_out[2] = (dv_acc[0] + dv_in[1].astype(jnp.float32)).astype(jnp.bfloat16)
+    dv_copy(2).start()
+
+    serve(0)
 
     x_wait(0)
     x_copy(4).start()
     x_wait(2)
     x_copy(5).start()
 
-    serve(0)
+    serve(1)
+    serve(2)
 
     local_copy(3).wait()
 
@@ -471,22 +489,22 @@
 
     turn(0)
 
-    for s in range(1, 4):
-        dv_copy(s).wait_recv()
-        dv_acc[...] += dv_in[s].astype(jnp.float32)
-
-    def gr_copy(s, half):
+    dv_copy(0).wait_recv()
+    dv_copy(2).wait_recv()
+    dv_low = (
+        dv_acc[1] + dv_in[0].astype(jnp.float32) + dv_in[2].astype(jnp.float32)
+    ).astype(jnp.bfloat16)
+
+    def gr_copy(slot, half):
         rows = pl.ds(half * 2 * ROWS, 2 * ROWS)
         return pltpu.make_async_remote_copy(
-            src_ref=gr_out.at[s, rows],
-            dst_ref=gr_in.at[s, rows],
-            send_sem=gr_send.at[half, s],
-            recv_sem=gr_recv.at[half, s],
-            device_id=at((j + s) % 4, g),
-            device_id_type=MESH,
-        )
-
-    dv_low = dv_acc[...].astype(jnp.bfloat16)
+            src_ref=gr_out.at[slot, rows],
+            dst_ref=gr_in.at[slot, rows],
+            send_sem=gr_send.at[half, slot],
+            recv_sem=gr_recv.at[half, slot],
+            device_id=at(across if slot == 2 else sibling, g),
+            device_id_type=MESH,
+        )
 
     def rows_of(quarter, i):
         first = pl.multiple_of((i * QUARTERS + quarter) * ROWS, 16)
@@ -494,12 +512,19 @@
 
     def spread(half):
         blocks = (2 * half, 2 * half + 1)
-        for s in range(1, 4):
+        rows = slice(half * 2 * ROWS, (half + 1) * 2 * ROWS)
+        for slot, quarter in ((1, diagonal), (0, sibling)):
             for i in blocks:
-                gr_out[s, i * ROWS : (i + 1) * ROWS] = rows_of((j + s) % 4, i).astype(jnp.bfloat16)
-            gr_copy(s, half).start()
-        for i in blocks:
-            gr_acc[i * ROWS : (i + 1) * ROWS] = rows_of(j, i)
+                gr_out[slot, i * ROWS : (i + 1) * ROWS] = rows_of(quarter, i).astype(jnp.bfloat16)
+            gr_copy(slot, half).start()
+        for slot, quarter in ((0, across), (1, j)):
+            for i in blocks:
+                gr_acc[slot, i * ROWS : (i + 1) * ROWS] = rows_of(quarter, i)
+        gr_copy(1, half).wait_recv()
+        gr_out[2, rows] = (gr_acc[0, rows] + gr_in[1, rows].astype(jnp.float32)).astype(
+            jnp.bfloat16
+        )
+        gr_copy(2, half).start()
 
     def own_copy(i):
         return pltpu.make_async_remote_copy(
@@ -513,10 +538,10 @@
 
     def deliver(half):
         rows = slice(half * 2 * ROWS, (half + 1) * 2 * ROWS)
-        total = gr_acc[rows]
-        for s in range(1, 4):
-            gr_copy(s, half).wait_recv()
-            total += gr_in[s, rows].astype(jnp.float32)
+        total = gr_acc[1, rows]
+        for slot in (0, 2):
+            gr_copy(slot, half).wait_recv()
+            total += gr_in[slot, rows].astype(jnp.float32)
         sum_out[rows] = total.astype(jnp.bfloat16)
         for i in (2 * half, 2 * half + 1):
             pl.when(g != i)(lambda: own_copy(i).start())
@@ -526,8 +551,6 @@
                 grad[i] = sum_out[i * ROWS : (i + 1) * ROWS]
 
     spread(0)
-    serve(1)
-    serve(2)
     turn(1)
     spread(1)
     deliver(0)
@@ -568,10 +591,10 @@
         for kind in range(3):
             group_copy(kind, s).wait_send()
 
-        key_copy(s).wait_send()
-        dv_copy(s).wait_send()
-        gr_copy(s, 0).wait_send()
-        gr_copy(s, 1).wait_send()
+        key_copy(s - 1).wait_send()
+        dv_copy(s - 1).wait_send()
+        gr_copy(s - 1, 0).wait_send()
+        gr_copy(s - 1, 1).wait_send()
         own_copy((g + s) % 4).wait_send()
     for route in range(6):
         x_copy(route).wait_send()
@@ -754,12 +777,12 @@
         pltpu.VMEM((QUARTERS, PART, GROUP_HEADS * PART), bf16),
         pltpu.VMEM((1, GROUP_HEADS * PART), f32),
         pltpu.VMEM((GROUP_HEADS * PART, HEAD_DIM), bf16),
-        pltpu.VMEM((PART, HEAD_DIM), f32),
-        pltpu.VMEM((4, PART, HEAD_DIM), bf16),
-        pltpu.VMEM((4, PART, HEAD_DIM), bf16),
-        pltpu.VMEM((4 * ROWS, HEAD_DIM), f32),
-        pltpu.VMEM((4, 4 * ROWS, HEAD_DIM), bf16),
-        pltpu.VMEM((4, 4 * ROWS, HEAD_DIM), bf16),
+        pltpu.VMEM((2, PART, HEAD_DIM), f32),
+        pltpu.VMEM((3, PART, HEAD_DIM), bf16),
+        pltpu.VMEM((3, PART, HEAD_DIM), bf16),
+        pltpu.VMEM((2, 4 * ROWS, HEAD_DIM), f32),
+        pltpu.VMEM((3, 4 * ROWS, HEAD_DIM), bf16),
+        pltpu.VMEM((3, 4 * ROWS, HEAD_DIM), bf16),
         pltpu.VMEM((4 * ROWS, HEAD_DIM), bf16),
         pltpu.VMEM((4, ROWS, HEAD_DIM), bf16),
     ]

time: 79.7 us -> 74.8 us (0.939)
  Pallas kernels: 77.5 us -> 72.7 us
    pallas_call x1, Pallas kernels: 76.2 us -> 71.3 us  [local(): pl.pallas_call(kernel, out_shape=(jax.ShapeDtypeStruct((4, ROWS, HEAD_DIM...]
where the time goes in v5:
time: 74.8 us; the launch traced here: 74.7 us
  Pallas kernels  72.7 us (97%)
  between operations  1.36 us (2%)
    pallas_call x1, Pallas kernels, local(): pl.pallas_call(kernel, out_shape=(jax.ShapeDtypeStruct((4, ROWS, HEAD_DIM...  71.3 us

profile of v5, /device:TPU:7, one launch (start us, length us, event | category | flops | bytes accessed | tf_op | source)
XLA Modules:
  0.0 74.7 jit_solution(6003224130741127583)
XLA Ops:
  0.6 0.0 copy-start.3
  0.6 0.6 copy-done.3
  1.3 0.0 copy-start
  1.3 0.0 copy-start.1
  1.3 0.0 copy-start.2
  1.3 71.3 %shard_map.103 = (bf16[4,112,256]{2,1,0:T(8,128)(2,1)S(1)}, bf16[8,336,128]{2,1,0:T(8,128)(2,1)S(1)}, s32[1]{0:T(128)}) custom-call(s32[32]{0:T(128)S(1)} %copy-done.3, bf16[128,1792]{1,0:T(8,128)(2,1)} %bitcast.19, bf16[128,2048]{1,0:T(8,128)(2,1)} %bitcast.17, bf16[128,1024]{1,0:T(8,128)(2,1)} %bitcast.22, bf16[128,2048]{1,0:T(8,128)(2,1)} %bitcast.18, ...), custom_call_target="tpu_custom_call" | custom-call | flops 3000000000 | bytes 6000000 | tf_op jit(solution)/shard_map/pallas_call | solution.py:804
  73.3 0.0 copy-done
  73.3 0.0 copy-done.1
  73.3 0.0 copy-done.2
  73.4 1.3 %conditional.1 = ((bf16[112,1024]{1,0:T(8,128)(2,1)}, f32[112,1024]{1,0:T(8,128)}, f32[112,1024]{1,0:T(8,128)})) conditional(s32[]{:T(128)} %bitcast.7, (bf16[4,112,256]{2,1,0:T(8,128)(2,1)S(1)}, bf16[8,336,128]{2,1,0:T(8,128)(2,1)S(1)}) %tuple.21, (s32[32]{0:T(128)S(1)}, bf16[112,1024]{1,0:T(8,128)(2,1)S(1)}, f32[112,1024]{1,0:T(8,128)S(1)}, ...), branch_computations={%region_0.0_spmd.clone, %region_1.0_spmd.clone} | conditional | bytes 8 | solution.py:858
  73.4 1.3 %branch_0_fun.1 = (bf16[112,1024]{1,0:T(8,128)(2,1)}, f32[112,1024]{1,0:T(8,128)}, f32[112,1024]{1,0:T(8,128)}) custom-call(bf16[4,112,256]{2,1,0:T(8,128)(2,1)S(1)} %get-tuple-element.50.grad, bf16[8,336,128]{2,1,0:T(8,128)(2,1)S(1)} %get-tuple-element.51.source), custom_call_target="tpu_custom_call" | custom-call | tf_op jit(solution)/shard_map/cond/branch_0_fun/pallas_call | solution.py:830
Async XLA Ops:
  0.6 0.7 copy-start.3
  1.3 72.0 %copy-start = (f32[1,112,1024]{2,1,0:T(8,128)S(1)}, f32[1,112,1024]{2,1,0:T(8,128)}, u32[]{:S(2)}) copy-start(f32[1,112,1024]{2,1,0:T(8,128)} %param.16) | copy-start | bytes 1376260
  1.3 72.0 %copy-start.1 = (f32[1,112,1024]{2,1,0:T(8,128)S(1)}, f32[1,112,1024]{2,1,0:T(8,128)}, u32[]{:S(2)}) copy-start(f32[1,112,1024]{2,1,0:T(8,128)} %param.17) | copy-start | bytes 1376260
  1.3 72.1 %copy-start.2 = (bf16[1,112,1024]{2,1,0:T(8,128)(2,1)S(1)}, bf16[1,112,1024]{2,1,0:T(8,128)(2,1)}, u32[]{:S(2)}) copy-start(bf16[1,112,1024]{2,1,0:T(8,128)(2,1)} %param.15) | copy-start | bytes 688132

commit v6 on v5

--- a/solution.py
+++ b/solution.py
@@ -37,7 +37,7 @@
 
 def kernel(
     winners, x_in, q_in, k_in, c_in, w_in, m_in, v_in,
-    grad_out, source_out, flag_out,
+    grad_out, source_out, flag_out, winners_out,
     k_all, q_g, c_g, x_g, x_t, expo, denom, cots,
     dv_acc, dv_out, dv_in, gr_acc, gr_out, gr_in, sum_out, grad,
     w_own, m_own, v_own, state, source, table_v, table_s,
@@ -140,10 +140,6 @@
 
     pl.semaphore_wait(barrier, 6 + 21)
 
-    for kind in range(3):
-        for s in range(1, 4):
-            group_copy(kind, s).start()
-
     for copy in state_copies:
         copy.wait()
     for band in range(8):
@@ -155,7 +151,7 @@
     core = mine % 2
     y = me // RING
     z = me % RING
-    starts, sizes = (0, 48, 80), (48, 32, 16)
+    starts, sizes = (0, 32, 80), (32, 48, 16)
     cuts = ((z + RING - 5) % RING, (z + RING - 10) % RING)
     reach = (5, 2)
 
@@ -282,6 +278,10 @@
     for part in range(3):
         deal(part)
 
+    for kind in range(3):
+        for s in range(1, 4):
+            group_copy(kind, s).start()
+
     right, left = (g + 1) % 4, (g + 3) % 4
     routes = ((0, g, right), (0, g, left), (1, g, left), (1, g, right), (0, left, right), (1, right, left))
     x_from = (left, right, right, left, left, right)
@@ -353,6 +353,11 @@
     for r in range(RING):
         most = jnp.maximum(most, jnp.sum(needed_by(r, 0)[2], axis=0, keepdims=True))
     flag_out[0] = jnp.max(jnp.where(most > SLOTS, 1, 0))
+
+    @pl.loop(0, MEMBERS)
+    def _(b):
+        winners_out[b] = winners[b]
+
     table_copy.wait()
 
     def key_copy(route):
@@ -381,6 +386,7 @@
     key_copy(1).start()
     key_copy(0).start()
 
+    swap(0)
     group_wait(1)
     denom[...] = jnp.zeros_like(denom)
 
@@ -405,7 +411,6 @@
                 denom[:, cols] += jnp.sum(e, axis=0, keepdims=True)
 
     scores(j)
-    swap(0)
 
     key_wait(1)
     key_copy(2).start()
@@ -794,22 +799,23 @@
     ]
     landing = pltpu.VMEM((8, 3 * ROWS, 128), bf16)
     parts = []
-    for rows in (48, 32, 16):
+    for rows in (32, 48, 16):
         for count in (16, SLOTS, SLOTS, 16):
             parts += [pltpu.VMEM((count, rows, 128), bf16)] * 2
-    parts += [pltpu.VMEM((30, rows, 128), bf16) for rows in (48, 32, 16)]
+    parts += [pltpu.VMEM((30, rows, 128), bf16) for rows in (32, 48, 16)]
     state_args = (weights[0], first_moment[0], second_moment[0])
     state_shape = jax.ShapeDtypeStruct((8, 3 * ROWS, 128), bf16)
     smem = pl.BlockSpec(memory_space=pltpu.SMEM)
-    grad, source, flag = pl.pallas_call(
+    grad, source, flag, same_winners = pl.pallas_call(
         kernel,
         out_shape=(
             jax.ShapeDtypeStruct((4, ROWS, HEAD_DIM), bf16),
             state_shape,
             jax.ShapeDtypeStruct((1,), jnp.int32),
+            jax.ShapeDtypeStruct((MEMBERS,), jnp.int32),
         ),
         in_specs=[smem] + [hbm] * 7,
-        out_specs=(hbm, hbm, smem),
+        out_specs=(hbm, hbm, smem, smem),
         scratch_shapes=scratch
         + own_state
         + [landing, pltpu.VMEM((8, 128), jnp.int32), pltpu.SMEM((8, 128), jnp.int32)]
@@ -852,7 +858,7 @@
             compiler_params=pltpu.CompilerParams(
                 collective_id=1, has_side_effects=True, vmem_limit_bytes=VMEM_LIMIT
             ),
-        )(winners, *state_args)
+        )(same_winners, *state_args)
         return step(grad, all_source)
 
     outs = lax.cond(flag[0] > 0, crowded, lambda: step(grad, source))

time: 74.8 us -> 72.3 us (0.967); the launches traced: 74.7 us -> 71 us
  Pallas kernels: 72.7 us -> 69.7 us
    pallas_call x1, Pallas kernels: 71.3 us -> 68.4 us  [local(): pl.pallas_call(kernel, out_shape=(jax.ShapeDtypeStruct((4, ROWS, HEAD_DIM...]
where the time goes in v6:
time: 72.3 us; the launch traced here: 71 us
  Pallas kernels  69.7 us (96%)
  between operations  1.25 us (2%)
    pallas_call x1, Pallas kernels, local(): pl.pallas_call(kernel, out_shape=(jax.ShapeDtypeStruct((4, ROWS, HEAD_DIM...  68.4 us

profile of v6, /device:TPU:7, one launch (start us, length us, event | category | flops | bytes accessed | tf_op | source)
XLA Modules:
  0.0 71.0 jit_solution(14790182098830687990)
XLA Ops:
  0.6 0.0 copy-start
  0.6 0.0 copy-start.1
  0.7 0.0 copy-start.2
  0.7 68.4 %shard_map.103 = (bf16[4,112,256]{2,1,0:T(8,128)(2,1)S(1)}, bf16[8,336,128]{2,1,0:T(8,128)(2,1)S(1)}, s32[1]{0:T(128)}, s32[32]{0:T(128)S(1)}) custom-call(s32[32]{0:T(128)} %winners.1, bf16[128,1792]{1,0:T(8,128)(2,1)} %bitcast.19, bf16[128,2048]{1,0:T(8,128)(2,1)} %bitcast.17, bf16[128,1024]{1,0:T(8,128)(2,1)} %bitcast.22, bf16[128,2048]{1,0:T(8,128)(2,1)} %bitcast.18, ...), custom_call_target="tpu_custom_call" | custom-call | flops 3000000000 | bytes 6000000 | tf_op jit(solution)/shard_map/pallas_call | solution.py:809
  69.6 0.0 copy-done
  69.6 0.0 copy-done.1
  69.7 0.0 copy-done.2
  69.7 1.3 %conditional.1 = ((bf16[112,1024]{1,0:T(8,128)(2,1)}, f32[112,1024]{1,0:T(8,128)}, f32[112,1024]{1,0:T(8,128)})) conditional(s32[]{:T(128)} %bitcast.7, (bf16[4,112,256]{2,1,0:T(8,128)(2,1)S(1)}, bf16[8,336,128]{2,1,0:T(8,128)(2,1)S(1)}) %tuple.21, (s32[32]{0:T(128)S(1)}, bf16[112,1024]{1,0:T(8,128)(2,1)S(1)}, f32[112,1024]{1,0:T(8,128)S(1)}, ...), branch_computations={%region_0.0_spmd.clone, %region_1.0_spmd.clone} | conditional | bytes 8 | solution.py:864
  69.7 1.3 %branch_0_fun.1 = (bf16[112,1024]{1,0:T(8,128)(2,1)}, f32[112,1024]{1,0:T(8,128)}, f32[112,1024]{1,0:T(8,128)}) custom-call(bf16[4,112,256]{2,1,0:T(8,128)(2,1)S(1)} %get-tuple-element.52.grad, bf16[8,336,128]{2,1,0:T(8,128)(2,1)S(1)} %get-tuple-element.53.source), custom_call_target="tpu_custom_call" | custom-call | tf_op jit(solution)/shard_map/cond/branch_0_fun/pallas_call | solution.py:836
Async XLA Ops:
  0.6 69.0 %copy-start = (f32[1,112,1024]{2,1,0:T(8,128)S(1)}, f32[1,112,1024]{2,1,0:T(8,128)}, u32[]{:S(2)}) copy-start(f32[1,112,1024]{2,1,0:T(8,128)} %param.16) | copy-start | bytes 1376260
  0.6 69.0 %copy-start.1 = (f32[1,112,1024]{2,1,0:T(8,128)S(1)}, f32[1,112,1024]{2,1,0:T(8,128)}, u32[]{:S(2)}) copy-start(f32[1,112,1024]{2,1,0:T(8,128)} %param.17) | copy-start | bytes 1376260
  0.7 69.0 %copy-start.2 = (bf16[1,112,1024]{2,1,0:T(8,128)(2,1)S(1)}, bf16[1,112,1024]{2,1,0:T(8,128)(2,1)}, u32[]{:S(2)}) copy-start(bf16[1,112,1024]{2,1,0:T(8,128)(2,1)} %param.15) | copy-start | bytes 688132

commit v7 on v6

--- a/solution.py
+++ b/solution.py
@@ -190,12 +190,13 @@
 
     def deal(part):
         @pl.loop(0, HALF)
-        def _(d):
+        def _(step):
             for role in range(2):
+                d = step if role == 0 else HALF - 1 - step
                 r = (z + RING - HALF * role - d) % RING
                 for row in range(2):
 
-                    def start(role=role, row=row, r=r):
+                    def start(role=role, row=row, r=r, d=d):
                         pltpu.make_async_remote_copy(
                             src_ref=place(state, r, part, row),
                             dst_ref=dealt[part][role].at[y * HALF + d],
@@ -249,7 +250,8 @@
                 swap_copy(part, 1 - role).wait_recv()
 
                 @pl.loop(0, HALF)
-                def _(d):
+                def _(step):
+                    d = step if role == 0 else HALF - 1 - step
                     for row in range(2):
                         member = row * RING + (z + RING - reach[role] + d) % RING
                         winner = winners[member]

time: 72.3 us -> 71.6 us (level); the launches traced: 71 us -> 71.3 us
  no operation moved by 1% of the time
where the time goes in v7:
time: 71.6 us; the launch traced here: 71.3 us
  Pallas kernels  70.1 us (98%)
  between operations  1.25 us (2%)
    pallas_call x1, Pallas kernels, local(): pl.pallas_call(kernel, out_shape=(jax.ShapeDtypeStruct((4, ROWS, HEAD_DIM...  68.7 us

profile of v7, /device:TPU:7, one launch (start us, length us, event | category | flops | bytes accessed | tf_op | source)
XLA Modules:
  0.0 71.3 jit_solution(13303608855596160099)
XLA Ops:
  0.6 0.0 copy-start
  0.6 0.0 copy-start.1
  0.7 0.0 copy-start.2
  0.7 68.7 %shard_map.103 = (bf16[4,112,256]{2,1,0:T(8,128)(2,1)S(1)}, bf16[8,336,128]{2,1,0:T(8,128)(2,1)S(1)}, s32[1]{0:T(128)}, s32[32]{0:T(128)S(1)}) custom-call(s32[32]{0:T(128)} %winners.1, bf16[128,1792]{1,0:T(8,128)(2,1)} %bitcast.19, bf16[128,2048]{1,0:T(8,128)(2,1)} %bitcast.17, bf16[128,1024]{1,0:T(8,128)(2,1)} %bitcast.22, bf16[128,2048]{1,0:T(8,128)(2,1)} %bitcast.18, ...), custom_call_target="tpu_custom_call" | custom-call | flops 3000000000 | bytes 6000000 | tf_op jit(solution)/shard_map/pallas_call | solution.py:811
  70.0 0.0 copy-done
  70.0 0.0 copy-done.1
  70.0 0.0 copy-done.2
  70.0 1.3 %conditional.1 = ((bf16[112,1024]{1,0:T(8,128)(2,1)}, f32[112,1024]{1,0:T(8,128)}, f32[112,1024]{1,0:T(8,128)})) conditional(s32[]{:T(128)} %bitcast.7, (bf16[4,112,256]{2,1,0:T(8,128)(2,1)S(1)}, bf16[8,336,128]{2,1,0:T(8,128)(2,1)S(1)}) %tuple.21, (s32[32]{0:T(128)S(1)}, bf16[112,1024]{1,0:T(8,128)(2,1)S(1)}, f32[112,1024]{1,0:T(8,128)S(1)}, ...), branch_computations={%region_0.0_spmd.clone, %region_1.0_spmd.clone} | conditional | bytes 8 | solution.py:866
  70.0 1.3 %branch_0_fun.1 = (bf16[112,1024]{1,0:T(8,128)(2,1)}, f32[112,1024]{1,0:T(8,128)}, f32[112,1024]{1,0:T(8,128)}) custom-call(bf16[4,112,256]{2,1,0:T(8,128)(2,1)S(1)} %get-tuple-element.52.grad, bf16[8,336,128]{2,1,0:T(8,128)(2,1)S(1)} %get-tuple-element.53.source), custom_call_target="tpu_custom_call" | custom-call | tf_op jit(solution)/shard_map/cond/branch_0_fun/pallas_call | solution.py:838
Async XLA Ops:
  0.6 69.3 %copy-start = (f32[1,112,1024]{2,1,0:T(8,128)S(1)}, f32[1,112,1024]{2,1,0:T(8,128)}, u32[]{:S(2)}) copy-start(f32[1,112,1024]{2,1,0:T(8,128)} %param.16) | copy-start | bytes 1376260
  0.6 69.3 %copy-start.1 = (f32[1,112,1024]{2,1,0:T(8,128)S(1)}, f32[1,112,1024]{2,1,0:T(8,128)}, u32[]{:S(2)}) copy-start(f32[1,112,1024]{2,1,0:T(8,128)} %param.17) | copy-start | bytes 1376260
  0.7 69.3 %copy-start.2 = (bf16[1,112,1024]{2,1,0:T(8,128)(2,1)S(1)}, bf16[1,112,1024]{2,1,0:T(8,128)(2,1)}, u32[]{:S(2)}) copy-start(bf16[1,112,1024]{2,1,0:T(8,128)(2,1)} %param.15) | copy-start | bytes 688132
